TPU v7x, 32 devices: a whole 2x2x4 slice. The times are simulated.
32 devices in a mesh: seg: 8 (over z, y), head: 4 (over x, core).
Axes of the slice: x: 2, y: 2, z: 4, core: 2. Of those that a mesh axis runs over, the one named last changes fastest.
Arguments:
- inputs: bfloat16 [16, 512, 1024], P('seg', None, 'head'), may hold values from -0.25 to 0.25
- cotangent: bfloat16 [16, 512, 1024], P('seg', None, 'head'), may hold values from -0.25 to 0.25
- state_in: bfloat16 [16, 512, 128], P('seg'), may hold values from -1.75 to 1.75
- state_out: bfloat16 [16, 512, 128], P('seg'), may hold values from -1.75 to 1.75
- log_decay: float32 [16, 16, 512], P('seg', 'head'), may hold values from -1 to 0
- parents: int32 [16], replicated, may hold values from -1 to 7, as said below
- slot_segment: int32 [16], replicated, may hold values from 0 to 15, as said below
Outputs:
- grad_inputs: bfloat16 [16, 512, 1024], P('seg', None, 'head')
- grad_state_in: float32 [16, 512, 128], P('seg', 'head')
- grad_state_out: float32 [16, 512, 128], P('seg', 'head')
Inputs may be any that keep to these rules, and one draw needn't show every extreme that they name: parents[s] is -1 for s < 2; each of the next 6 segments has a parent below 2; every other segment has a parent from 2 to 7; every segment below 8 has a child. `slot_segment`: each segment is held in exactly one slot.
All inputs are finite; a program needn't handle non-finite values.
Results may differ from a plain program's by a relative error of at most 0.0085.
Values sent between devices are 32-bit elements; how exact they have to be, the bound alone decides.
No kernel may reach another device: no remote copies, remote signals or barrier semaphores. Data moves between devices by JAX's collectives and lax.ppermute only.
A program may use at most 64 MiB of HBM per device.

v0:
```python
import jax
import jax.numpy as jnp
from jax import lax
from jax.sharding import PartitionSpec as P

ROOTS = 2
MIDS = 6


def causal_decay(cumulative):
    length = cumulative.shape[1]
    later = jnp.arange(length)[:, None] >= jnp.arange(length)[None, :]
    spread = cumulative[:, :, None] - cumulative[:, None, :]
    return jnp.where(later[None], jnp.exp(jnp.where(later[None], spread, 0.0)), 0.0)


def local_terms(sliced):
    inputs_s, cotan_s, sin_s, sout_s, decay_s = sliced
    length = inputs_s.shape[0]
    head_count = decay_s.shape[0]
    head_width = inputs_s.shape[1] // head_count
    cumulative = jnp.cumsum(decay_s, axis=1)
    to_end = jnp.exp(cumulative[:, -1:] - cumulative)
    from_start = jnp.exp(cumulative)
    input_heads = inputs_s.reshape(length, head_count, head_width)
    cotan_heads = cotan_s.reshape(length, head_count, head_width)
    scaled_in = (input_heads.astype(jnp.float32) * to_end.T[:, :, None]).astype(jnp.bfloat16)
    scaled_cot = (cotan_heads.astype(jnp.float32) * from_start.T[:, :, None]).astype(jnp.bfloat16)
    local_end = jnp.einsum("lhp,ln->hpn", scaled_in, sin_s, preferred_element_type=jnp.float32)
    local_adj = jnp.einsum("lhp,ln->hpn", scaled_cot, sout_s, preferred_element_type=jnp.float32)
    scores = jnp.dot(sout_s, sin_s.T, preferred_element_type=jnp.float32)
    decay_mask = causal_decay(cumulative)
    weights = (decay_mask * scores[None]).astype(jnp.bfloat16)
    quad_in = jnp.einsum("htu,thp->uhp", weights, cotan_heads, preferred_element_type=jnp.float32)
    products = jnp.einsum(
        "thp,uhp->htu", cotan_heads, input_heads, preferred_element_type=jnp.float32
    )
    coupled = (decay_mask * products).astype(jnp.bfloat16)
    write_quad = jnp.einsum("htu,tn->un", coupled, sout_s, preferred_element_type=jnp.float32)
    read_quad = jnp.einsum("htu,un->tn", coupled, sin_s, preferred_element_type=jnp.float32)
    return (quad_in, write_quad, read_quad, local_end, local_adj, to_end, from_start)


def gather_rows(flags, states):
    return jnp.einsum("sk,shpn->khpn", flags, states, precision=lax.Precision.HIGHEST)


def spread_rows(flags, table):
    return jnp.einsum("sk,khpn->shpn", flags, table, precision=lax.Precision.HIGHEST)


def split_product(form, data, table):
    upper = table.astype(jnp.bfloat16)
    lower = (table - upper.astype(jnp.float32)).astype(jnp.bfloat16)
    first = jnp.einsum(form, data, upper, preferred_element_type=jnp.float32)
    return first + jnp.einsum(form, data, lower, preferred_element_type=jnp.float32)


def shards(inputs, cotangent, state_in, state_out, log_decay, parents, slot_segment):
    seg_dev = inputs.shape[0]
    length = inputs.shape[1]
    head_count = log_decay.shape[1]
    head_width = inputs.shape[2] // head_count
    slot_count = slot_segment.shape[0]
    quad_in, write_quad, read_quad, local_end, local_adj, to_end, from_start = lax.map(
        local_terms, (inputs, cotangent, state_in, state_out, log_decay)
    )
    end_decay = jnp.exp(jnp.sum(log_decay, axis=2))
    decay_four = end_decay[:, :, None, None]
    first_slot = lax.axis_index("seg") * seg_dev
    owned_ids = lax.dynamic_slice_in_dim(slot_segment, first_slot, seg_dev)
    everyone = jnp.arange(slot_count, dtype=jnp.int32)
    owned_parent = jnp.sum(
        jnp.where(owned_ids[:, None] == everyone[None, :], parents[None, :], 0), axis=1
    )
    parent_count = ROOTS + MIDS
    parent_ids = jnp.arange(parent_count, dtype=jnp.int32)
    holds_row = (owned_ids[:, None] == parent_ids[None, :]).astype(jnp.float32)
    child_of = (owned_parent[:, None] == parent_ids[None, :]).astype(jnp.float32)
    root_table = lax.psum(gather_rows(holds_row[:, :ROOTS], local_end), "seg")
    start_mid = spread_rows(child_of[:, :ROOTS], root_table)
    mid_table = lax.psum(
        gather_rows(holds_row[:, ROOTS:], decay_four * start_mid + local_end), "seg"
    )
    start_state = start_mid + spread_rows(child_of[:, ROOTS:], mid_table)
    mid_adj = lax.psum(gather_rows(child_of[:, ROOTS:], local_adj), "seg")
    end_mid = spread_rows(holds_row[:, ROOTS:], mid_adj)
    root_adj = lax.psum(gather_rows(child_of[:, :ROOTS], local_adj + decay_four * end_mid), "seg")
    adjoint_end = end_mid + spread_rows(holds_row[:, :ROOTS], root_adj)
    input_heads = inputs.reshape(seg_dev, length, head_count, head_width)
    cotan_heads = cotangent.reshape(seg_dev, length, head_count, head_width)
    end_weight = jnp.transpose(to_end, (0, 2, 1))
    start_weight = jnp.transpose(from_start, (0, 2, 1))
    state_in_term = end_weight[..., None] * split_product("sun,shpn->suhp", state_in, adjoint_end)
    grad_inputs = (
        (quad_in + state_in_term)
        .astype(jnp.bfloat16)
        .reshape(seg_dev, length, head_count * head_width)
    )
    write_state = jnp.sum(
        end_weight[..., None] * split_product("suhp,shpn->suhn", input_heads, adjoint_end), axis=2
    )
    read_state = jnp.sum(
        start_weight[..., None] * split_product("sthp,shpn->sthn", cotan_heads, start_state), axis=2
    )
    grad_state_in, grad_state_out = (
        lax.psum_scatter(write_quad + write_state, "head", scatter_dimension=1, tiled=True),
        lax.psum_scatter(read_quad + read_state, "head", scatter_dimension=1, tiled=True),
    )
    return (grad_inputs, grad_state_in, grad_state_out)


def solution(mesh):
    placed = (
        P("seg", None, "head"),
        P("seg", None, "head"),
        P("seg", None, None),
        P("seg", None, None),
        P("seg", "head", None),
        P(),
        P(),
    )
    return jax.shard_map(
        shards,
        mesh=mesh,
        in_specs=placed,
        out_specs=(P("seg", None, "head"), P("seg", "head", None), P("seg", "head", None)),
        check_vma=False,
    )
```

profile of v0, /device:TPU:0, one launch (start us, length us, event | category | flops | bytes accessed | tf_op | source)
XLA Modules:
  0.0 282.6 jit_solution(410634210412469638)
XLA Ops:
  11.6 32.4 %while.22 = (s32[]{:T(128)}, f32[2,512,4,64]{1,3,2,0:T(8,128)}, f32[2,512,128]{1,2,0:T(8,128)}, f32[2,512,128]{1,2,0:T(8,128)S(1)}, f32[2,4,64,128]{3,0,2,1:T(2,...) while((s32[]{:T(128)}, f32[2,512,4,64]{1,3,2,0:T(8,128)}, ...), condition=%wide.region_4.5_spmd, body=%wide.region_0.4_spmd.sunk | while | flops 550508608 | bytes 22753060 | solution.py:65
  15.4 2.6 dynamic_update_slice.40
  18.3 4.2 %dynamic_update_slice.41 = f32[2,4,64,128]{3,0,2,1:T(2,128)} dynamic-update-slice(f32[2,4,64,128]{3,0,2,1:T(2,128)} %get-tuple-element.319, f32[1,4,64,128]{3,0,2,1:T(1,128)S(1)} %bitcast.206, s32[]{:T(128)S(6)} %copy.194, s32[]{:T(128)} %constant.30.clone.1..sunk, s32[]{:T(128)} %constant.30.clone.1..sunk, s32[]{:T(128)} %constant.30.clone.1..sunk) | dynamic-update-slice | bytes 262148 | tf_op jit(solution)/shard_map/while/body/jit(dynamic_update_index_in_dim)/dynamic_update_slice | solution.py:65
  22.5 1.5 convert_reduce_fusion.2
  25.2 1.6 fusion.132
  31.7 2.6 dynamic_update_slice.40
  34.5 4.2 %dynamic_update_slice.41 = f32[2,4,64,128]{3,0,2,1:T(2,128)} dynamic-update-slice(f32[2,4,64,128]{3,0,2,1:T(2,128)} %get-tuple-element.319, f32[1,4,64,128]{3,0,2,1:T(1,128)S(1)} %bitcast.206, s32[]{:T(128)S(6)} %copy.194, s32[]{:T(128)} %constant.30.clone.1..sunk, s32[]{:T(128)} %constant.30.clone.1..sunk, s32[]{:T(128)} %constant.30.clone.1..sunk) | dynamic-update-slice | bytes 262148 | tf_op jit(solution)/shard_map/while/body/jit(dynamic_update_index_in_dim)/dynamic_update_slice | solution.py:65
  38.7 1.5 convert_reduce_fusion.2
  41.4 1.6 fusion.132
  44.0 1.4 fusion.49
  45.4 2.8 fusion.58
  49.2 85.7 %all-reduce.7.cloned.1.call-done = (f32[6,4,64,128]{3,0,2,1:T(8,128)}, f32[2,4,64,128]{3,0,2,1:T(2,128)}) async-done(((f32[6,4,64,128]{3,0,2,1:T(8,128)}, f32[2,4,64,128]{3,0,2,1:T(2,128)}), (f32[6,4,64,128]{3,0,2,1:T(8,128)}, f32[2,4,64,128]{3,0,2,1:T(2,128)})) %all-reduce.7.cloned.1.call-update) | async-done | bytes 1048592 | tf_op jit(solution)/shard_map/psum | solution.py:86
  134.9 1.8 fusion.54
  136.7 1.5 fusion.60
  138.3 1.6 fusion.41
  139.8 1.8 fusion.38
  141.9 82.8 %all-reduce.5.cloned.1.call-done = (f32[2,4,64,128]{3,0,2,1:T(2,128)}, f32[6,4,64,128]{3,0,2,1:T(8,128)}) async-done(((f32[2,4,64,128]{3,0,2,1:T(2,128)}, f32[6,4,64,128]{3,0,2,1:T(8,128)}), (f32[2,4,64,128]{3,0,2,1:T(2,128)}, f32[6,4,64,128]{3,0,2,1:T(8,128)})) %all-reduce.5.cloned.1.call-update) | async-done | bytes 1048592 | tf_op jit(solution)/shard_map/psum | solution.py:88
  224.8 1.5 fusion.51
  226.9 1.4 fusion.30
  230.4 1.3 fusion.29
  235.2 15.0 %reduce-scatter.3.cloned.1.call-done = f32[2,128,128]{1,2,0:T(8,128)} async-done(((f32[2,512,128]{1,2,0:T(8,128)}), f32[2,128,128]{1,2,0:T(8,128)}) %reduce-scatter.3.cloned.1.call-update) | async-done | bytes 131088 | tf_op jit(solution)/shard_map/reduce_scatter | solution.py:107
  250.2 1.7 copy.105
  251.8 22.5 %reduce-scatter.5.cloned.1.call-done = f32[2,128,128]{1,2,0:T(8,128)} async-done(((f32[2,512,128]{1,2,0:T(8,128)}), f32[2,128,128]{1,2,0:T(8,128)}) %reduce-scatter.5.cloned.1.call-update) | async-done | bytes 131088 | tf_op jit(solution)/shard_map/reduce_scatter | solution.py:108
  274.4 1.7 copy.106
  (105 shorter events, 24.0 us)
Async XLA Ops:
  7.2 4.4 %copy-start = (bf16[2,512,128]{2,1,0:T(8,128)(2,1)S(1)}, bf16[2,512,128]{2,1,0:T(8,128)(2,1)}, u32[]{:S(2)}) copy-start(bf16[2,512,128]{2,1,0:T(8,128)(2,1)} %param.11) | copy-start | bytes 786436
  7.2 4.4 %copy-start.1 = (bf16[2,512,128]{2,1,0:T(8,128)(2,1)S(1)}, bf16[2,512,128]{2,1,0:T(8,128)(2,1)}, u32[]{:S(2)}) copy-start(bf16[2,512,128]{2,1,0:T(8,128)(2,1)} %param.12) | copy-start | bytes 786436
  7.2 127.7 %all-reduce.7.cloned.1.call-start = ((), (), s32[]{:S(2)}) async-start(), calls=%async_computation.5 | async-start | bytes 2621440 | tf_op jit(solution)/shard_map/psum | solution.py:86
  22.5 1.8 copy-start.8
  24.0 1.2 copy-start.2
  24.6 2.2 copy-start.9
  26.8 1.0 copy-start.3
  38.7 1.8 copy-start.8
  40.2 1.2 copy-start.2
  40.8 2.2 copy-start.9
  43.0 1.0 copy-start.3
  44.0 92.7 %copy-start.6 = (f32[2,512,128]{1,2,0:T(8,128)}, f32[2,512,128]{1,2,0:T(8,128)S(1)}, u32[]{:S(2)}) copy-start(f32[2,512,128]{1,2,0:T(8,128)S(1)} %get-tuple-element.80) | copy-start | bytes 1572868
  45.4 92.8 %copy-start.11 = (f32[2,4,64,128]{3,0,2,1:T(2,128)S(1)}, f32[2,4,64,128]{3,0,2,1:T(2,128)}, u32[]{:S(2)}) copy-start(f32[2,4,64,128]{3,0,2,1:T(2,128)} %get-tuple-element.78) | copy-start | bytes 786436
  48.2 176.5 %all-reduce.5.cloned.1.call-start = ((), (), s32[]{:S(2)}) async-start(), calls=%async_computation.4 | async-start | bytes 2621440 | tf_op jit(solution)/shard_map/psum | solution.py:88
  141.7 108.5 %reduce-scatter.3.cloned.1.call-start = ((), (), s32[]{:S(2)}) async-start(), calls=%async_computation.2 | async-start | bytes 655360 | tf_op jit(solution)/shard_map/reduce_scatter | solution.py:107
  226.8 1.4 copy-start.10
  226.9 2.4 copy-start.5
  229.2 45.2 %reduce-scatter.5.cloned.1.call-start = ((), (), s32[]{:S(2)}) async-start(), calls=%async_computation.3 | async-start | bytes 655360 | tf_op jit(solution)/shard_map/reduce_scatter | solution.py:108
  230.4 1.4 copy-start.7
  231.7 1.4 copy-start.4
Sparse Core Ops, SparseCore 0:
  48.4 86.4 all-reduce.6
  141.8 82.9 all-reduce.4
  229.3 20.8 reduce-scatter.2
  252.7 21.6 reduce-scatter.4
where the time goes:
time: 284 us; the launch traced here: 283 us
  waiting for transfers between devices  206 us (73%)
  matrix products  26.9 us (9%)
  local copies, waits for them, and re-layouts  26.3 us (9%)
  between operations  14 us (5%)
  other arithmetic  8.63 us (3%)
    psum x1, waiting for transfers between devices, shards(): mid_adj = lax.psum(gather_rows(child_of[:, ROOTS:], local_adj), 'seg')  85.7 us
    psum x1, waiting for transfers between devices, shards(): lax.psum(gather_rows(child_of[:, :ROOTS], local_adj + decay_four * end_mi...  82.8 us
    reduce_scatter x1, waiting for transfers between devices, shards(): lax.psum_scatter(read_quad + read_state, 'head', scatter_dimension=1, til...  22.5 us
    reduce_scatter x1, waiting for transfers between devices, shards(): lax.psum_scatter(write_quad + write_state, 'head', scatter_dimension=1, t...  15 us
    dynamic_update_slice x4, local copies, waits for them, and re-layouts, shards(): lax.map(local_terms, (inputs, cotangent, state_in, state_out, log_decay))  13.6 us
    dot_general x4, matrix products, gather_rows(): jnp.einsum('sk,shpn->khpn', flags, states, precision=lax.Precision.HIGHEST)  7.56 us
  transfers between devices with their start and end apart: 4, of which 4 were waited for; matrix products, arithmetic and copies ran while one was open for 3% of the time, Pallas kernels for 0%

commit v1 on v0

v1 whole, which is shorter than its diff:
```python
import functools

import jax
import jax.numpy as jnp
from jax import lax
from jax.experimental import pallas as pl
from jax.experimental.pallas import tpu as pltpu
from jax.sharding import PartitionSpec as P

ROOTS = 2
MIDS = 6
PARENTS = ROOTS + MIDS
BLOCK = 128
F32 = jnp.float32
BF16 = jnp.bfloat16


def dot(a, b, dims):
    return lax.dot_general(a, b, (dims, ((), ())), preferred_element_type=F32)


NN = ((1,), (0,))
NT = ((1,), (1,))
TN = ((0,), (0,))


def two_parts(x):
    upper = x.astype(BF16).astype(F32)
    return jnp.concatenate([upper, x - upper], axis=0).astype(BF16)


def head_columns(rows, seg, heads, width):
    row = lax.broadcasted_iota(jnp.int32, (2 * rows, width), 0) % rows
    col = lax.broadcasted_iota(jnp.int32, (2 * rows, width), 1) // (width // heads)
    return (row == seg * heads + col).astype(BF16)


def rows_of(chain, order, rel, count):
    me = lax.axis_index("seg")
    first = jnp.bitwise_and(jnp.right_shift(me, order[0]), 1)
    second = jnp.bitwise_and(jnp.right_shift(me, order[1]), 1)
    part = jnp.bitwise_xor(first * 2 + second, rel)
    return pl.multiple_of((chain * 4 + part) * count, count)


def local_kernel(orders, in_hbm, cot_hbm, sin_hbm, sout_hbm, decay_hbm,
                 scin_ref, sccot_ref, cum_ref, toend_ref, decays_ref, *refs):
    states_s, in_ref, cot_ref, sin_ref, sout_ref, decay_ref, sems = refs[-7:]
    copies = [
        pltpu.make_async_copy(src, dst, sems.at[i])
        for i, (src, dst) in enumerate((
            (decay_hbm, decay_ref), (in_hbm, in_ref), (sin_hbm, sin_ref),
            (cot_hbm, cot_ref), (sout_hbm, sout_ref),
        ))
    ]
    for copy in copies:
        copy.start()
    segs, _, width = in_ref.shape
    heads, length = decay_ref.shape[1:]
    rows = segs * heads
    copies[0].wait()
    decay = jnp.concatenate([decay_ref[s] for s in range(segs)], axis=0)
    p0 = decay.astype(BF16).astype(F32)
    r0 = decay - p0
    p1 = r0.astype(BF16).astype(F32)
    pieces = jnp.concatenate([p0, p1, r0 - p1], axis=0).astype(BF16)
    tri = (
        lax.broadcasted_iota(jnp.int32, (BLOCK, BLOCK), 0)
        <= lax.broadcasted_iota(jnp.int32, (BLOCK, BLOCK), 1)
    ).astype(BF16)
    before = jnp.zeros((rows, 1), F32)
    parts = []
    for b in range(length // BLOCK):
        sums = dot(pieces[:, b * BLOCK:(b + 1) * BLOCK], tri, NN)
        part = sums[:rows] + sums[rows:2 * rows] + sums[2 * rows:] + before
        before = part[:, BLOCK - 1:]
        parts.append(part)
    cum = jnp.concatenate(parts, axis=1)
    cum_ref[...] = cum
    row = lax.broadcasted_iota(jnp.int32, (rows, width), 0)
    col = lax.broadcasted_iota(jnp.int32, (rows, width), 1) // (width // heads)
    for s in range(segs):
        of_head = jnp.where(row == s * heads + col, jnp.exp(before), 0.0)
        decays_ref[s:s + 1] = jnp.sum(of_head, axis=0, keepdims=True)
    to_end = two_parts(jnp.exp(before - cum))
    toend_ref[...] = to_end
    from_start = two_parts(jnp.exp(cum))
    for i, (src, scaled_ref, factor, state_ref) in enumerate((
        (in_ref, scin_ref, to_end, sin_ref), (cot_ref, sccot_ref, from_start, sout_ref)
    )):
        copies[2 * i + 1].wait()
        for s in range(segs):
            spread = dot(factor, head_columns(rows, s, heads, width), TN)
            scaled_ref[s] = (src[s].astype(F32) * spread).astype(BF16)
        copies[2 * i + 2].wait()
        for s in range(segs):
            states_s[i * segs + s] = dot(state_ref[s], scaled_ref[s], TN)
    for c, order in enumerate(orders):
        near_ref, away_ref = refs[2 * c:2 * c + 2]
        count = near_ref.shape[2]
        for rel in range(4):
            place = rows_of(c, order, rel, count)
            for i in range(2 * segs):
                (near_ref, away_ref)[rel // 2][rel % 2, i] = states_s[i, pl.ds(place, count)]


def quad_kernel(seg, heads, in_ref, cot_ref, sin_ref, sout_ref, cum_ref, quad_ref, write_ref, read_ref):
    _, length, width = in_ref.shape
    pairs = width // BLOCK
    per = heads // pairs
    cum = cum_ref[...]
    cum_col = jnp.transpose(cum)
    scores = dot(sin_ref[0], sout_ref[0], NT)
    lane = lax.broadcasted_iota(jnp.int32, (length, BLOCK), 1) // (BLOCK // per)
    masked_cot = []
    for h in range(heads):
        pair = cot_ref[0, :, (h // per) * BLOCK:(h // per + 1) * BLOCK]
        masked_cot.append(jnp.where(lane == h % per, pair, jnp.zeros_like(pair)))
    causal = (
        lax.broadcasted_iota(jnp.int32, (BLOCK, BLOCK), 1)
        >= lax.broadcasted_iota(jnp.int32, (BLOCK, BLOCK), 0)
    )
    for u in range(0, length, BLOCK):
        coupled = None
        quads = [None] * pairs
        for h in range(heads):
            g = h // per
            row = seg * heads + h
            spread = cum[row:row + 1, u:] - cum_col[u:u + BLOCK, row:row + 1]
            decay = jnp.exp(spread)
            near = jnp.where(causal, decay[:, :BLOCK], 0.0)
            decay = near if u + BLOCK == length else jnp.concatenate([near, decay[:, BLOCK:]], axis=1)
            weights = (decay * scores[u:u + BLOCK, u:]).astype(BF16)
            part = dot(weights, masked_cot[h][u:], NN)
            quads[g] = part if quads[g] is None else quads[g] + part
            products = dot(in_ref[0, u:u + BLOCK, g * BLOCK:(g + 1) * BLOCK], masked_cot[h][u:], NT)
            coupled = decay * products if coupled is None else coupled + decay * products
        for g in range(pairs):
            quad_ref[u:u + BLOCK, g * BLOCK:(g + 1) * BLOCK] = quads[g]
        coupled = coupled.astype(BF16)
        write_ref[u:u + BLOCK] = dot(coupled, sout_ref[0, u:], NN)
        back = dot(coupled, sin_ref[0, u:u + BLOCK], TN)
        if u == 0:
            read_ref[...] = back
        else:
            read_ref[u:] += back


def plan_kernel(step_count, parents_ref, slots_ref, near_ref, grand_ref, hold_ref, up_ref, far_ref,
                flag_ref, at_ref, owner_s, slot_s):
    width = near_ref.shape[2]
    group = near_ref.shape[0]
    segs = group // 4
    count = slots_ref.shape[0] // segs
    me = lax.axis_index("seg")

    def note(j, carry):
        seg = slots_ref[j]

        @pl.when(seg < PARENTS)
        def _():
            owner_s[seg] = j // segs
            slot_s[seg] = j % segs

        return carry

    lax.fori_loop(0, slots_ref.shape[0], note, 0)

    def put(ref, i, j, value):
        ref[i, j:j + 1] = jnp.broadcast_to(value.astype(F32), (1, width))

    ids, above, top = [], [], []
    for j in range(group):
        seg = slots_ref[jnp.bitwise_xor(me, j // segs) * segs + j % segs]
        up = parents_ref[seg]
        known = jnp.maximum(up, 0)
        ids.append(seg)
        above.append(up)
        top.append(jnp.where(up >= 0, parents_ref[known], -1))
        away = jnp.bitwise_xor(owner_s[known], me)
        low, mid = jnp.bitwise_and(away, 1), jnp.bitwise_and(jnp.right_shift(away, 1), 1)
        row = (mid * (count // 2) + low * (count // 4) + jnp.right_shift(away, 2)) * segs + slot_s[known]
        at_ref[j:j + 1] = jnp.broadcast_to(row.astype(jnp.int32), (1, width))
    for j in range(group):
        for p in range(PARENTS):
            put(near_ref, j, p, above[j] == p)
            put(grand_ref, j, p, top[j] == p)
            put(hold_ref, j, p, ids[j] == p)
        for i in range(group):
            put(up_ref, j, i, above[j] == ids[i])
            put(far_ref, j, i, top[j] == ids[i])
    for p in range(PARENTS):
        away = jnp.bitwise_xor(owner_s[p], me)
        for k in range(step_count):
            high = jnp.right_shift(away, 2 + k)
            put(flag_ref, k, p, high == 0)
            put(flag_ref, step_count + k, p, high == 1)


def parent_decays(at_ref, decay_refs):
    decays = jnp.concatenate([ref[...] for ref in decay_refs], axis=0)
    row = lax.broadcasted_iota(jnp.int32, decays.shape, 0)
    return [
        jnp.sum(jnp.where(row == at_ref[j:j + 1], decays, 0.0), axis=0, keepdims=True)
        for j in range(at_ref.shape[0])
    ]


def raw_states(order, near_ref, first_ref, second_ref, segs, count):
    ends, adjs = [None] * (4 * segs), [None] * (4 * segs)
    for place, device in enumerate((0, 1 << order[0], 1 << order[1], 3)):
        for s in range(segs):
            for kind, found in ((0, ends), (1, adjs)):
                i = kind * segs + s
                if place < 2:
                    value = (near_ref, first_ref)[place][0, i]
                else:
                    at = ((place - 2) * 2 * segs + i) * count
                    value = second_ref[at:at + count]
                found[device * segs + s] = value
    return ends, adjs


def cross_kernel(order, step, near_p, grand_p, hold_p, flag_ref, at_ref, mine_ref, tail_ref,
                 near_ref, first_ref, second_ref, *refs):
    later, out_ref = refs[:-1], refs[-1]
    group = near_p.shape[0]
    segs = group // 4
    count = out_ref.shape[1]
    steps = flag_ref.shape[0] // 2
    decay = parent_decays(at_ref, (mine_ref, tail_ref))
    ends, adjs = raw_states(order, near_ref, first_ref, second_ref, segs, count)
    as_end = flag_ref[step]
    from_end = [as_end * hold_p[j] for j in range(group)]
    from_adj = [(1.0 - as_end) * (near_p[j] + grand_p[j] * decay[j]) for j in range(group)]
    passed = [
        jnp.where((as_end < 0.5) | (flag_ref[steps + j] > 0.5), 1.0, 0.0) for j in range(len(later))
    ]
    for p in range(PARENTS):
        value = 0.0
        for j in range(group):
            value += from_end[j][p:p + 1] * ends[j] + from_adj[j][p:p + 1] * adjs[j]
        for flag, got in zip(passed, later):
            value += flag[p:p + 1] * got[p]
        out_ref[p] = value


def finish_kernel(order, near_p, grand_p, hold_p, up_ref, far_ref, flag_ref, at_ref, mine_ref, tail_ref,
                  near_ref, first_ref, second_ref, *refs):
    later, (own_ref, there_ref, away_ref) = refs[:-3], refs[-3:]
    group = near_p.shape[0]
    segs = group // 4
    count = own_ref.shape[1]
    steps = flag_ref.shape[0] // 2
    decay = parent_decays(at_ref, (mine_ref, tail_ref))
    ends, adjs = raw_states(order, near_ref, first_ref, second_ref, segs, count)
    values, known = [], []
    for p in range(PARENTS):
        value, end = 0.0, 0.0
        for j, got in enumerate(later):
            value += got[p]
            end += flag_ref[steps + j, p:p + 1] * got[p]
        values.append(value)
        known.append(end)
    link = [up_ref[j] + far_ref[j] * decay[j] for j in range(group)]
    for place, device in enumerate((0, 1 << order[0], 1 << order[1], 3)):
        out_ref, base = ((own_ref, 0), (there_ref, 0), (away_ref, 0), (away_ref, 2 * segs))[place]
        for s in range(segs):
            j = device * segs + s
            weight = near_p[j] + grand_p[j] * decay[j]
            start, adj = 0.0, 0.0
            for i in range(group):
                start += link[j][i:i + 1] * ends[i]
                adj += link[i][j:j + 1] * adjs[i]
            for p in range(PARENTS):
                start += weight[p:p + 1] * known[p]
                adj += hold_p[j, p:p + 1] * values[p]
            out_ref[base + s] = start
            out_ref[base + segs + s] = adj


def state_kernel(orders, scin_ref, sccot_ref, *refs):
    parts, refs = refs[:3 * len(orders)], refs[3 * len(orders):]
    segs = scin_ref.shape[0]
    quads, refs = refs[:2 * segs], refs[2 * segs:]
    keep_w, send_w, keep_r, send_r, adj_out, start_s, total_s = refs
    for c, order in enumerate(orders):
        own, fourth, fifth = parts[3 * c:3 * c + 3]
        count = own.shape[1]
        for rel, (ref, base) in enumerate(((own, 0), (fourth, 0), (fifth, 0), (fifth, 2 * segs))):
            place = rows_of(c, order, rel, count)
            for s in range(segs):
                start_s[s, pl.ds(place, count)] = ref[base + s].astype(BF16)
                adj_out[s, pl.ds(place, count)] = ref[base + segs + s].astype(BF16)
    bit = lax.axis_index("head") % 2
    piece = keep_w.shape[2]
    for a, (scaled, table, keep_ref, send_ref) in enumerate(
        ((scin_ref, adj_out, keep_w, send_w), (sccot_ref, start_s, keep_r, send_r))
    ):
        for s in range(segs):
            total_s[a, s] = quads[2 * s + a][...] + dot(scaled[s], table[s], NT)
            for x in range(2):
                mine = pl.multiple_of((2 * x + bit) * piece, piece)
                other = pl.multiple_of((2 * x + 1 - bit) * piece, piece)
                keep_ref[x, s] = total_s[a, s, pl.ds(mine, piece)]
                send_ref[x, s] = total_s[a, s, pl.ds(other, piece)]


def inputs_kernel(sin_ref, toend_ref, adj_ref, *refs):
    quads, gin_ref = refs[:-1], refs[-1]
    segs, _, width = gin_ref.shape
    rows = toend_ref.shape[0] // 2
    for s in range(segs):
        to_end = dot(toend_ref[...], head_columns(rows, s, rows // segs, width), TN)
        gin_ref[s] = (quads[s][...] + to_end * dot(sin_ref[s], adj_ref[s], NN)).astype(BF16)


def whole(*shape):
    return pl.BlockSpec(shape, lambda *_: (0,) * len(shape))


def in_vmem():
    return pl.BlockSpec(memory_space=pltpu.VMEM)


def in_smem():
    return pl.BlockSpec(memory_space=pltpu.SMEM)


def flip(x, axis, count, bit):
    return lax.ppermute(x, axis, [(i, i ^ (1 << bit)) for i in range(count)])


PARAMS = pltpu.CompilerParams(vmem_limit_bytes=48 * 1024 * 1024)


def close_decays(decays, count):
    bits = count.bit_length() - 1
    if bits == 3:
        other, across, both = (
            lax.ppermute(decays, "seg", [(i, i ^ k) for i in range(count)]) for k in (1, 4, 5)
        )
        return jnp.concatenate([decays, across, other, both], axis=0)
    for bit in range(2, bits):
        decays = jnp.concatenate([decays, flip(decays, "seg", count, bit)], axis=0)
    return jnp.concatenate([decays, flip(decays, "seg", count, 0)], axis=0)


def tree_chain(order, count, plan, decays, near, near_late, first, second):
    near_p, grand_p, hold_p, up, far, flags, at = plan
    shape = near.shape[1:]
    part = jax.ShapeDtypeStruct(shape, F32)
    later = []
    for k in range(2, len(order)):
        send = pl.pallas_call(
            functools.partial(cross_kernel, order, k - 2),
            out_shape=jax.ShapeDtypeStruct((PARENTS, *shape[1:]), F32),
            in_specs=[in_vmem()] * (10 + len(later)),
            out_specs=in_vmem(),
            compiler_params=PARAMS,
            cost_estimate=pl.CostEstimate(flops=2_000_000, bytes_accessed=500_000, transcendentals=0),
            name="across_step",
        )(near_p, grand_p, hold_p, flags, at, *decays, near, first, second, *later)
        later.append(flip(send, "seg", count, order[k]))
    own, there, away = pl.pallas_call(
        functools.partial(finish_kernel, order),
        out_shape=(part, part, jax.ShapeDtypeStruct((2 * shape[0], *shape[1:]), F32)),
        in_specs=[in_vmem()] * (12 + len(later)),
        out_specs=(in_vmem(), in_vmem(), in_vmem()),
        compiler_params=PARAMS,
        cost_estimate=pl.CostEstimate(flops=2_000_000, bytes_accessed=500_000, transcendentals=0),
        name="finish_part",
    )(near_p, grand_p, hold_p, up, far, flags, at, *decays, near_late, first, second, *later)
    fourth = flip(away, "seg", count, order[1])
    fifth = flip(jnp.concatenate([there, fourth[shape[0]:]], axis=0), "seg", count, order[0])
    return own, fourth, fifth


def shards(mesh_sizes, inputs, cotangent, state_in, state_out, log_decay, parents, slot_segment):
    count = mesh_sizes["seg"]
    head_devices = mesh_sizes["head"]
    bit_count = count.bit_length() - 1
    segs, length, width = inputs.shape
    heads = log_decay.shape[1]
    state = state_in.shape[2]
    rows = segs * heads
    orders = [[0, 1] + list(range(2, bit_count)), [1, 0] + list(range(2, bit_count))]
    part_rows = state // (4 * len(orders))

    whole_in = whole(segs, length, width)
    whole_state = whole(segs, length, state)
    scaled = jax.ShapeDtypeStruct((segs, length, width), BF16)
    raw = jax.ShapeDtypeStruct((2, 2 * segs, part_rows, width), F32)
    scaled_in, scaled_cot, cum, to_end, decays, *raws = pl.pallas_call(
        functools.partial(local_kernel, orders),
        out_shape=(
            scaled, scaled,
            jax.ShapeDtypeStruct((rows, length), F32),
            jax.ShapeDtypeStruct((2 * rows, length), BF16),
            jax.ShapeDtypeStruct((segs, width), F32),
            *[raw] * (2 * len(orders)),
        ),
        in_specs=[pl.BlockSpec(memory_space=pltpu.HBM)] * 5,
        out_specs=tuple([in_vmem()] * (5 + 2 * len(orders))),
        scratch_shapes=[
            pltpu.VMEM((2 * segs, state, width), F32),
            pltpu.VMEM(inputs.shape, BF16),
            pltpu.VMEM(inputs.shape, BF16),
            pltpu.VMEM(state_in.shape, BF16),
            pltpu.VMEM(state_in.shape, BF16),
            pltpu.VMEM(log_decay.shape, F32),
            pltpu.SemaphoreType.DMA((5,)),
        ],
        compiler_params=PARAMS,
        cost_estimate=pl.CostEstimate(flops=200_000_000, bytes_accessed=4_000_000, transcendentals=8192),
        name="local_states",
    )(inputs, cotangent, state_in, state_out, log_decay)
    nears, aways = raws[0::2], raws[1::2]

    quads = []
    for s in range(segs):
        pick = lambda *_, s=s: (s, 0, 0)
        quads.append(
            pl.pallas_call(
                functools.partial(quad_kernel, s, heads),
                grid=(1,),
                out_shape=(
                    jax.ShapeDtypeStruct((length, width), F32),
                    jax.ShapeDtypeStruct((length, state), F32),
                    jax.ShapeDtypeStruct((length, state), F32),
                ),
                in_specs=[
                    pl.BlockSpec((1, length, width), pick),
                    pl.BlockSpec((1, length, width), pick),
                    pl.BlockSpec((1, length, state), pick),
                    pl.BlockSpec((1, length, state), pick),
                    whole(rows, length),
                ],
                out_specs=(whole(length, width), whole(length, state), whole(length, state)),
                compiler_params=PARAMS,
                cost_estimate=pl.CostEstimate(
                    flops=4_000_000_000, bytes_accessed=2_000_000, transcendentals=heads * length * length
                ),
                name="quadratic_part",
            )(inputs, cotangent, state_in, state_out, cum)
        )

    firsts = [flip(away, "seg", count, order[0]) for away, order in zip(aways, orders)]
    mine = close_decays(decays, count)
    held, quads[0] = lax.optimization_barrier((nears[0], quads[0]))
    late, quads[1:] = lax.optimization_barrier((nears[0], quads[1:]))
    raw_rows = 2 * segs * part_rows
    seconds = []
    for c, order in enumerate(orders):
        message = [(held if c == 0 else nears[c])[1].reshape(raw_rows, width), firsts[c][1].reshape(raw_rows, width)]
        if c == 0:
            message.append(mine)
        seconds.append(flip(jnp.concatenate(message, axis=0), "seg", count, order[1]))
    decays = (mine, seconds[0][2 * raw_rows:])

    group = 4 * segs
    by_parent = jax.ShapeDtypeStruct((group, PARENTS, width), F32)
    by_segment = jax.ShapeDtypeStruct((group, group, width), F32)
    plan = pl.pallas_call(
        functools.partial(plan_kernel, bit_count - 2),
        out_shape=(
            by_parent, by_parent, by_parent, by_segment, by_segment,
            jax.ShapeDtypeStruct((2 * (bit_count - 2), PARENTS, width), F32),
            jax.ShapeDtypeStruct((group, width), jnp.int32),
        ),
        in_specs=[in_smem(), in_smem()],
        out_specs=tuple([in_vmem()] * 7),
        scratch_shapes=[pltpu.SMEM((PARENTS,), jnp.int32), pltpu.SMEM((PARENTS,), jnp.int32)],
        compiler_params=PARAMS,
        cost_estimate=pl.CostEstimate(flops=2_000_000, bytes_accessed=500_000, transcendentals=0),
        name="plan_tree",
    )(parents, slot_segment)

    parts = []
    for c, order in enumerate(orders):
        last = late if c == 0 else nears[c]
        parts.extend(tree_chain(order, count, plan, decays, nears[c], last, firsts[c], seconds[c]))

    piece = length // head_devices
    half = jax.ShapeDtypeStruct((2, segs, piece, state), F32)
    keep_w, send_w, keep_r, send_r, adj_all = pl.pallas_call(
        functools.partial(state_kernel, orders),
        out_shape=(half, half, half, half, jax.ShapeDtypeStruct((segs, state, width), BF16)),
        in_specs=[in_vmem()] * (2 + len(parts) + 2 * segs),
        out_specs=tuple([in_vmem()] * 5),
        scratch_shapes=[
            pltpu.VMEM((segs, state, width), BF16),
            pltpu.VMEM((2, segs, length, state), F32),
        ],
        compiler_params=PARAMS,
        cost_estimate=pl.CostEstimate(flops=200_000_000, bytes_accessed=8_000_000, transcendentals=0),
        name="state_terms",
    )(scaled_in, scaled_cot, *parts, *[part for quad in quads for part in quad[1:]])

    grad_inputs = pl.pallas_call(
        inputs_kernel,
        out_shape=scaled,
        in_specs=[in_vmem()] * (3 + segs),
        out_specs=in_vmem(),
        compiler_params=PARAMS,
        cost_estimate=pl.CostEstimate(flops=200_000_000, bytes_accessed=8_000_000, transcendentals=0),
        name="grad_inputs",
    )(state_in, to_end, adj_all, *[quad[0] for quad in quads])

    place = lax.axis_index("head") // 2
    outs = []
    for keep, send in ((keep_w, send_w), (keep_r, send_r)):
        both = keep + flip(send, "head", head_devices, 0)
        away = lax.dynamic_index_in_dim(both, 1 - place, axis=0, keepdims=False)
        here = lax.dynamic_index_in_dim(both, place, axis=0, keepdims=False)
        outs.append(here + flip(away, "head", head_devices, 1))
    return grad_inputs, outs[0], outs[1]


def solution(mesh):
    sizes = {name: int(mesh.shape[name]) for name in ("seg", "head")}
    placed = (
        P("seg", None, "head"),
        P("seg", None, "head"),
        P("seg", None, None),
        P("seg", None, None),
        P("seg", "head", None),
        P(),
        P(),
    )
    return jax.shard_map(
        functools.partial(shards, sizes),
        mesh=mesh,
        in_specs=placed,
        out_specs=(P("seg", None, "head"), P("seg", "head", None), P("seg", "head", None)),
        check_vma=False,
    )
```

time: 284 us -> 60.5 us (0.21)
  waiting for transfers between devices: 206 us -> 22.4 us
  matrix products: 26.9 us -> 0 us
  local copies, waits for them, and re-layouts: 26.3 us -> 5.39 us
  starting transfers between devices: 0.34 us -> 19.3 us
  between operations: 14 us -> 0.87 us
  Pallas kernels: 0 us -> 10.8 us
  other arithmetic: 8.63 us -> 1.44 us
    psum x2 -> x0, waiting for transfers between devices: 169 us -> none  [the longest x1 85.7 us: shards(): mid_adj = lax.psum(gather_rows(child_of[:, ROOTS:], local_adj), 'seg')]
    reduce_scatter x2 -> x0, waiting for transfers between devices: 37.5 us -> none  [the longest x1 22.5 us: shards(): lax.psum_scatter(read_quad + read_state, 'head', scatter_dimension=1, til...]
    dot_general x28 -> x0, matrix products: 26.9 us -> none  [the longest x4 7.56 us: gather_rows(): jnp.einsum('sk,shpn->khpn', flags, states, precision=lax.Precision.HIGHEST)]
    ppermute x0 -> x17, waiting for transfers between devices: none -> 22.4 us  [the longest x14 22.4 us: flip(): return lax.ppermute(x, axis, [(i, i ^ 1 << bit) for i in range(count)])]
    ppermute x0 -> x17, starting transfers between devices: none -> 19.3 us  [the longest x14 13.6 us: flip(): return lax.ppermute(x, axis, [(i, i ^ 1 << bit) for i in range(count)])]
    dynamic_update_slice x4 -> x0, local copies, waits for them, and re-layouts: 13.6 us -> none  [shards(): lax.map(local_terms, (inputs, cotangent, state_in, state_out, log_decay))]
    pallas_call x0 -> x10, Pallas kernels: none -> 10.8 us  [the longest x2 4.03 us: shards(): pl.pallas_call(functools.partial(quad_kernel, s, heads), grid=(1,), out_s...]
    while x22 -> x0, local copies, waits for them, and re-layouts: 5.36 us -> none
  transfers between devices with their start and end apart: 4 -> 17, of which waited for: 4 -> 10; matrix products, arithmetic and copies ran while one was open for 3% -> 1% of each run, Pallas kernels for 0% -> 13%
where the time goes in v1:
time: 60.5 us; the launch traced here: 60.2 us
  waiting for transfers between devices  22.4 us (37%)
  starting transfers between devices  19.3 us (32%)
  Pallas kernels  10.8 us (18%)
  local copies, waits for them, and re-layouts  5.39 us (9%)
  other arithmetic  1.44 us (2%)
  between operations  0.87 us (1%)
    ppermute x14, waiting for transfers between devices, flip(): return lax.ppermute(x, axis, [(i, i ^ 1 << bit) for i in range(count)])  22.4 us
    ppermute x14, starting transfers between devices, flip(): return lax.ppermute(x, axis, [(i, i ^ 1 << bit) for i in range(count)])  13.6 us
    ppermute x3, starting transfers between devices, close_decays(): lax.ppermute(decays, 'seg', [(i, i ^ k) for i in range(count)])  5.7 us
    unnamed x26, local copies, waits for them, and re-layouts  5.29 us
    pallas_call x2, Pallas kernels, shards(): pl.pallas_call(functools.partial(quad_kernel, s, heads), grid=(1,), out_s...  4.03 us
    pallas_call x1, Pallas kernels, shards(): pl.pallas_call(functools.partial(local_kernel, orders), out_shape=(scaled...  1.76 us
    add x2, other arithmetic, shards(): outs.append(here + flip(away, 'head', head_devices, 1))  1.34 us
    pallas_call x1, Pallas kernels, shards(): pl.pallas_call(functools.partial(state_kernel, orders), out_shape=(half,...  1.3 us
  transfers between devices with their start and end apart: 17, of which 10 were waited for; matrix products, arithmetic and copies ran while one was open for 1% of the time, Pallas kernels for 13%

profile of v1, /device:TPU:0, one launch (start us, length us, event | category | flops | bytes accessed | tf_op | source)
XLA Modules:
  0.0 60.2 jit_solution(5761438897278960617)
XLA Ops:
  1.6 1.0 %copy-done.2 = bf16[2,512,256]{2,1,0:T(8,128)(2,1)S(1)} copy-done((bf16[2,512,256]{2,1,0:T(8,128)(2,1)S(1)}, bf16[2,512,256]{2,1,0:T(8,128)(2,1)}, u32[]{:S(2)}) %copy-start.2) | copy-done | bytes 524312
  2.6 1.0 %copy-done.4 = bf16[2,512,256]{2,1,0:T(8,128)(2,1)S(1)} copy-done((bf16[2,512,256]{2,1,0:T(8,128)(2,1)S(1)}, bf16[2,512,256]{2,1,0:T(8,128)(2,1)}, u32[]{:S(2)}) %copy-start.4) | copy-done | bytes 524312
  5.3 1.8 %local_states.1 = (bf16[2,512,256]{2,1,0:T(8,128)(2,1)S(1)}, bf16[2,512,256]{2,1,0:T(8,128)(2,1)S(1)}, f32[8,512]{1,0:T(8,128)S(1)}, bf16[16,512]{1,0:T(8,128)(2...) custom-call(bf16[2,512,256]{2,1,0:T(8,128)(2,1)S(1)} %copy-done.2, ...), custom_call_target="tpu_custom_call" | custom-call | flops 200000000 | bytes 4000000 | tf_op jit(solution)/shard_map/local_states/pallas_call | solution.py:394
  7.1 5.1 %collective-permute-start.2 = (f32[2,256]{1,0:T(2,128)S(1)}, f32[2,256]{1,0:T(2,128)S(1)}, u32[]{:S(2)}, u32[]{:S(2)}) collective-permute-start(f32[2,256]{1,0:T(2,128)S(1)} %get-tuple-element.54), channel_id=1, source_target_pairs={{0,20},{4,16},{8,28},{12,24},{16,4},{20,0},{24,12},{28,8},{1,21},{... | collective-permute-start | bytes 6152 | tf_op jit(solution)/shard_map/ppermute | solution.py:341
  12.8 1.7 %collective-permute-start.3 = (f32[2,4,16,256]{3,2,1,0:T(8,128)S(1)}, f32[2,4,16,256]{3,2,1,0:T(8,128)S(1)}, u32[]{:S(2)}, u32[]{:S(2)}) collective-permute-start(f32[2,4,16,256]{3,2,1,0:T(8,128)S(1)} %get-tuple-element.61), channel_id=1, source_target_pairs={{0,4},{4,0},{8,12},{12,8},{16,20},{20,16},{24,28},{28,24},{1,5},{5... | collective-permute-start | bytes 393224 | tf_op jit(solution)/shard_map/ppermute | solution.py:331
  14.5 1.6 %collective-permute-start.8 = (f32[2,4,16,256]{3,2,1,0:T(8,128)S(1)}, f32[2,4,16,256]{3,2,1,0:T(8,128)S(1)}, u32[]{:S(2)}, u32[]{:S(2)}) collective-permute-start(f32[2,4,16,256]{3,2,1,0:T(8,128)S(1)} %get-tuple-element.70), channel_id=1, source_target_pairs={{0,8},{4,12},{8,0},{12,4},{16,24},{20,28},{24,16},{28,20},{1,9},{5... | collective-permute-start | bytes 393224 | tf_op jit(solution)/shard_map/ppermute | solution.py:331
  16.1 2.0 %quadratic_part.2 = (f32[512,256]{1,0:T(8,128)S(1)}, f32[512,128]{1,0:T(8,128)S(1)}, f32[512,128]{1,0:T(8,128)S(1)}) custom-call(bf16[2,512,256]{2,1,0:T(8,128)(2,1)S(1)} %copy-done.2, bf16[2,512,256]{2,1,0:T(8,128)(2,1)S(1)} %copy-done.4, bf16[2,512,128]{2,1,0:T(8,128)(2,1)S(1)} %copy-done, bf16[2,512,128]{2,1,0:T(8,128)(2,1)S(1)} %copy-done.6, ...), custom_call_target="tpu_custom_call" | custom-call | flops 4000000000 | bytes 2000000 | tf_op jit(solution)/shard_map/quadratic_part/pallas_call | solution.py:424
  19.8 1.6 %collective-permute-start.9 = (f32[128,256]{1,0:T(8,128)S(1)}, f32[128,256]{1,0:T(8,128)S(1)}, u32[]{:S(2)}, u32[]{:S(2)}) collective-permute-start(f32[128,256]{1,0:T(8,128)S(1)} %pad_maximum_fusion.1), channel_id=1, source_target_pairs={{0,4},{4,0},{8,12},{12,8},{16,20},{20,16},{24,28},{28,24},{1,5},{5... | collective-permute-start | bytes 393224 | tf_op jit(solution)/shard_map/ppermute | solution.py:331
  21.4 1.2 %plan_tree.1 = (f32[8,8,256]{2,1,0:T(8,128)S(1)}, f32[8,8,256]{2,1,0:T(8,128)S(1)}, f32[8,8,256]{2,1,0:T(8,128)S(1)}, f32[8,8,256]{2,1,0:T(8,128)S(1)}, f32[8,8,...) custom-call(s32[16]{0:T(128)S(1)} %copy-done.11, s32[16]{0:T(128)S(1)} %copy-done.12), custom_call_target="tpu_custom_call" | custom-call | flops 2000000 | bytes 500000 | tf_op jit(solution)/shard_map/plan_tree/pallas_call | solution.py:464
  22.5 1.3 %collective-permute-done.4.second_ref = f32[136,256]{1,0:T(8,128)S(1)} collective-permute-done((f32[136,256]{1,0:T(8,128)S(1)}, f32[136,256]{1,0:T(8,128)S(1)}, u32[]{:S(2)}, u32[]{:S(2)}) %collective-permute-start.4) | collective-permute-done | bytes 139296 | tf_op jit(solution)/shard_map/ppermute | solution.py:331
  24.1 2.9 %collective-permute-start.5 = (f32[8,16,256]{2,1,0:T(8,128)S(1)}, f32[8,16,256]{2,1,0:T(8,128)S(1)}, u32[]{:S(2)}, u32[]{:S(2)}) collective-permute-start(f32[8,16,256]{2,1,0:T(8,128)S(1)} %across_step.2), channel_id=1, source_target_pairs={{0,16},{4,20},{8,24},{12,28},{16,0},{20,4},{24,8},{28,12},{1,17},{... | collective-permute-start | bytes 393224 | tf_op jit(solution)/shard_map/ppermute | solution.py:331
  27.7 2.0 %quadratic_part.3 = (f32[512,256]{1,0:T(8,128)S(1)}, f32[512,128]{1,0:T(8,128)S(1)}, f32[512,128]{1,0:T(8,128)S(1)}) custom-call(bf16[2,512,256]{2,1,0:T(8,128)(2,1)S(1)} %copy-done.3, bf16[2,512,256]{2,1,0:T(8,128)(2,1)S(1)} %copy-done.5, bf16[2,512,128]{2,1,0:T(8,128)(2,1)S(1)} %copy-done.1, bf16[2,512,128]{2,1,0:T(8,128)(2,1)S(1)} %copy-done.7, ...), custom_call_target="tpu_custom_call" | custom-call | flops 4000000000 | bytes 2000000 | tf_op jit(solution)/shard_map/quadratic_part/pallas_call | solution.py:424
  29.8 5.1 %collective-permute-done.5.refs_0_ = f32[8,16,256]{2,1,0:T(8,128)S(1)} collective-permute-done((f32[8,16,256]{2,1,0:T(8,128)S(1)}, f32[8,16,256]{2,1,0:T(8,128)S(1)}, u32[]{:S(2)}, u32[]{:S(2)}) %collective-permute-start.5) | collective-permute-done | bytes 131104 | tf_op jit(solution)/shard_map/ppermute | solution.py:331
  35.3 1.0 %collective-permute-done.10.refs_0_ = f32[8,16,256]{2,1,0:T(8,128)S(1)} collective-permute-done((f32[8,16,256]{2,1,0:T(8,128)S(1)}, f32[8,16,256]{2,1,0:T(8,128)S(1)}, u32[]{:S(2)}, u32[]{:S(2)}) %collective-permute-start.10) | collective-permute-done | bytes 131104 | tf_op jit(solution)/shard_map/ppermute | solution.py:331
  37.3 2.9 %collective-permute-done.6.refs_1_ = f32[8,16,256]{2,1,0:T(8,128)S(1)} collective-permute-done((f32[8,16,256]{2,1,0:T(8,128)S(1)}, f32[8,16,256]{2,1,0:T(8,128)S(1)}, u32[]{:S(2)}, u32[]{:S(2)}) %collective-permute-start.6) | collective-permute-done | bytes 131104 | tf_op jit(solution)/shard_map/ppermute | solution.py:331
  40.9 2.1 %collective-permute-done.11.refs_4_ = f32[8,16,256]{2,1,0:T(8,128)S(1)} collective-permute-done((f32[8,16,256]{2,1,0:T(8,128)S(1)}, f32[8,16,256]{2,1,0:T(8,128)S(1)}, u32[]{:S(2)}, u32[]{:S(2)}) %collective-permute-start.11) | collective-permute-done | bytes 131104 | tf_op jit(solution)/shard_map/ppermute | solution.py:331
  43.6 1.8 %collective-permute-done.7.refs_2_ = f32[8,16,256]{2,1,0:T(8,128)S(1)} collective-permute-done((f32[8,16,256]{2,1,0:T(8,128)S(1)}, f32[8,16,256]{2,1,0:T(8,128)S(1)}, u32[]{:S(2)}, u32[]{:S(2)}) %collective-permute-start.7) | collective-permute-done | bytes 131104 | tf_op jit(solution)/shard_map/ppermute | solution.py:331
  45.3 2.7 %collective-permute-done.12.refs_5_ = f32[8,16,256]{2,1,0:T(8,128)S(1)} collective-permute-done((f32[8,16,256]{2,1,0:T(8,128)S(1)}, f32[8,16,256]{2,1,0:T(8,128)S(1)}, u32[]{:S(2)}, u32[]{:S(2)}) %collective-permute-start.12) | collective-permute-done | bytes 131104 | tf_op jit(solution)/shard_map/ppermute | solution.py:331
  48.0 1.3 %state_terms.1 = (f32[2,2,128,128]{3,2,1,0:T(8,128)S(1)}, f32[2,2,128,128]{3,2,1,0:T(8,128)}, f32[2,2,128,128]{3,2,1,0:T(8,128)S(1)}, f32[2,2,128,128]{3,2,1,0:T(8,128)}, bf16[2,128,256]{2,1,0:T(8,128)(2,1)S(1)}) custom-call(bf16[2,512,256]{2,1,0:T(8,128)(2,1)S(1)} %get-tuple-element.45.scin_ref, bf16[2,512,256]{2,1,0:T(8,128)(2,1)S(1)} %get-tuple-element.46.sccot_ref, ...), custom_call_target="tpu_custom_call" | custom-call | flops 200000000 | bytes 8000000 | tf_op jit(solution)/shard_map/state_terms/pallas_call | solution.py:486
  49.8 1.2 %collective-permute-done.13 = f32[2,2,128,128]{3,2,1,0:T(8,128)S(1)} collective-permute-done((f32[2,2,128,128]{3,2,1,0:T(8,128)}, f32[2,2,128,128]{3,2,1,0:T(8,128)S(1)}, u32[]{:S(2)}, u32[]{:S(2)}) %collective-permute-start.13) | collective-permute-done | bytes 262176 | tf_op jit(solution)/shard_map/ppermute | solution.py:331
  51.1 1.6 %collective-permute-start.14 = (f32[2,128,128]{2,1,0:T(8,128)S(1)}, f32[2,128,128]{2,1,0:T(8,128)S(1)}, u32[]{:S(2)}, u32[]{:S(2)}) collective-permute-start(f32[2,128,128]{2,1,0:T(8,128)S(1)} %dynamic-slice_bitcast_fusion.1), channel_id=1, source_target_pairs={{0,2},{1,3},{2,0},{3,1},{4,6},{5,7},{6,4},{7,5},{8,10},{9,11},{10,... | collective-permute-start | bytes 393224 | tf_op jit(solution)/shard_map/ppermute | solution.py:331
  52.7 1.2 %grad_inputs.1 = bf16[2,512,256]{2,1,0:T(8,128)(2,1)} custom-call(bf16[2,512,128]{2,1,0:T(8,128)(2,1)S(1)} %copy-done.1, bf16[16,512]{1,0:T(8,128)(2,1)S(1)} %get-tuple-element.44.toend_ref, bf16[2,128,256]{2,1,0:T(8,128)(2,1)S(1)} %get-tuple-element.78.adj_ref, f32[512,256]{1,0:T(8,128)S(1)} %get-tuple-element.79.refs_0_, ...), custom_call_target="tpu_custom_call" | custom-call | flops 200000000 | bytes 8000000 | tf_op jit(solution)/shard_map/grad_inputs/pallas_call | solution.py:500
  54.6 2.3 %collective-permute-done.14 = f32[2,128,128]{2,1,0:T(8,128)S(1)} collective-permute-done((f32[2,128,128]{2,1,0:T(8,128)S(1)}, f32[2,128,128]{2,1,0:T(8,128)S(1)}, u32[]{:S(2)}, u32[]{:S(2)}) %collective-permute-start.14) | collective-permute-done | bytes 131104 | tf_op jit(solution)/shard_map/ppermute | solution.py:331
  57.5 2.0 %collective-permute-done.16 = f32[2,128,128]{2,1,0:T(8,128)S(1)} collective-permute-done((f32[2,128,128]{2,1,0:T(8,128)S(1)}, f32[2,128,128]{2,1,0:T(8,128)S(1)}, u32[]{:S(2)}, u32[]{:S(2)}) %collective-permute-start.16) | collective-permute-done | bytes 131104 | tf_op jit(solution)/shard_map/ppermute | solution.py:331
  (64 shorter events, 11.0 us)
Async XLA Ops:
  7.1 11.1 %collective-permute-start.2 = (f32[2,256]{1,0:T(2,128)S(1)}, f32[2,256]{1,0:T(2,128)S(1)}, u32[]{:S(2)}, u32[]{:S(2)}) collective-permute-start(f32[2,256]{1,0:T(2,128)S(1)} %get-tuple-element.54), channel_id=1, source_target_pairs={{0,20},{4,16},{8,28},{12,24},{16,4},{20,0},{24,12},{28,8},{1,21},{... | collective-permute-start | bytes 6152 | tf_op jit(solution)/shard_map/ppermute | solution.py:341
  12.2 6.0 %collective-permute-start.1 = (f32[2,256]{1,0:T(2,128)S(1)}, f32[2,256]{1,0:T(2,128)S(1)}, u32[]{:S(2)}, u32[]{:S(2)}) collective-permute-start(f32[2,256]{1,0:T(2,128)S(1)} %get-tuple-element.54), channel_id=1, source_target_pairs={{0,4},{4,0},{8,12},{12,8},{16,20},{20,16},{24,28},{28,24},{1,5},{5... | collective-permute-start | bytes 6152 | tf_op jit(solution)/shard_map/ppermute | solution.py:341
  12.7 5.5 %collective-permute-start = (f32[2,256]{1,0:T(2,128)S(1)}, f32[2,256]{1,0:T(2,128)S(1)}, u32[]{:S(2)}, u32[]{:S(2)}) collective-permute-start(f32[2,256]{1,0:T(2,128)S(1)} %get-tuple-element.54), channel_id=1, source_target_pairs={{0,16},{4,20},{8,24},{12,28},{16,0},{20,4},{24,8},{28,12},{1,17},{... | collective-permute-start | bytes 6152 | tf_op jit(solution)/shard_map/ppermute | solution.py:341
  12.8 5.3 %collective-permute-start.3 = (f32[2,4,16,256]{3,2,1,0:T(8,128)S(1)}, f32[2,4,16,256]{3,2,1,0:T(8,128)S(1)}, u32[]{:S(2)}, u32[]{:S(2)}) collective-permute-start(f32[2,4,16,256]{3,2,1,0:T(8,128)S(1)} %get-tuple-element.61), channel_id=1, source_target_pairs={{0,4},{4,0},{8,12},{12,8},{16,20},{20,16},{24,28},{28,24},{1,5},{5... | collective-permute-start | bytes 393224 | tf_op jit(solution)/shard_map/ppermute | solution.py:331
  14.5 5.2 %collective-permute-start.8 = (f32[2,4,16,256]{3,2,1,0:T(8,128)S(1)}, f32[2,4,16,256]{3,2,1,0:T(8,128)S(1)}, u32[]{:S(2)}, u32[]{:S(2)}) collective-permute-start(f32[2,4,16,256]{3,2,1,0:T(8,128)S(1)} %get-tuple-element.70), channel_id=1, source_target_pairs={{0,8},{4,12},{8,0},{12,4},{16,24},{20,28},{24,16},{28,20},{1,9},{5... | collective-permute-start | bytes 393224 | tf_op jit(solution)/shard_map/ppermute | solution.py:331
  18.2 3.1 %copy-start.11 = (s32[16]{0:T(128)S(1)}, s32[16]{0:T(128)}, u32[]{:S(2)}) copy-start(s32[16]{0:T(128)} %parents_ref.1) | copy-start | bytes 196
  18.2 3.1 %copy-start.12 = (s32[16]{0:T(128)S(1)}, s32[16]{0:T(128)}, u32[]{:S(2)}) copy-start(s32[16]{0:T(128)} %slots_ref.1) | copy-start | bytes 196
  18.8 5.1 %collective-permute-start.4 = (f32[136,256]{1,0:T(8,128)S(1)}, f32[136,256]{1,0:T(8,128)S(1)}, u32[]{:S(2)}, u32[]{:S(2)}) collective-permute-start(f32[136,256]{1,0:T(8,128)S(1)} %concatenate.17), channel_id=1, source_target_pairs={{0,8},{4,12},{8,0},{12,4},{16,24},{20,28},{24,16},{28,20},{1,9},{5... | collective-permute-start | bytes 417800 | tf_op jit(solution)/shard_map/ppermute | solution.py:331
  19.7 8.0 %copy-start.7 = (bf16[2,512,128]{2,1,0:T(8,128)(2,1)S(1)}, bf16[2,512,128]{2,1,0:T(8,128)(2,1)}, u32[]{:S(2)}) copy-start(bf16[2,512,128]{2,1,0:T(8,128)(2,1)} %sout_ref.3) | copy-start | bytes 786436
  19.8 7.3 %collective-permute-start.9 = (f32[128,256]{1,0:T(8,128)S(1)}, f32[128,256]{1,0:T(8,128)S(1)}, u32[]{:S(2)}, u32[]{:S(2)}) collective-permute-start(f32[128,256]{1,0:T(8,128)S(1)} %pad_maximum_fusion.1), channel_id=1, source_target_pairs={{0,4},{4,0},{8,12},{12,8},{16,20},{20,16},{24,28},{28,24},{1,5},{5... | collective-permute-start | bytes 393224 | tf_op jit(solution)/shard_map/ppermute | solution.py:331
  23.9 3.8 %copy-start.3 = (bf16[2,512,256]{2,1,0:T(8,128)(2,1)S(1)}, bf16[2,512,256]{2,1,0:T(8,128)(2,1)}, u32[]{:S(2)}) copy-start(bf16[2,512,256]{2,1,0:T(8,128)(2,1)} %in_ref.3) | copy-start | bytes 1572868
  23.9 3.8 %copy-start.5 = (bf16[2,512,256]{2,1,0:T(8,128)(2,1)S(1)}, bf16[2,512,256]{2,1,0:T(8,128)(2,1)}, u32[]{:S(2)}) copy-start(bf16[2,512,256]{2,1,0:T(8,128)(2,1)} %cot_ref.3) | copy-start | bytes 1572868
  24.1 3.6 %copy-start.1 = (bf16[2,512,128]{2,1,0:T(8,128)(2,1)S(1)}, bf16[2,512,128]{2,1,0:T(8,128)(2,1)}, u32[]{:S(2)}) copy-start(bf16[2,512,128]{2,1,0:T(8,128)(2,1)} %sin_ref.5) | copy-start | bytes 786436
  24.1 10.7 %collective-permute-start.5 = (f32[8,16,256]{2,1,0:T(8,128)S(1)}, f32[8,16,256]{2,1,0:T(8,128)S(1)}, u32[]{:S(2)}, u32[]{:S(2)}) collective-permute-start(f32[8,16,256]{2,1,0:T(8,128)S(1)} %across_step.2), channel_id=1, source_target_pairs={{0,16},{4,20},{8,24},{12,28},{16,0},{20,4},{24,8},{28,12},{1,17},{... | collective-permute-start | bytes 393224 | tf_op jit(solution)/shard_map/ppermute | solution.py:331
  27.3 9.1 %collective-permute-start.10 = (f32[8,16,256]{2,1,0:T(8,128)S(1)}, f32[8,16,256]{2,1,0:T(8,128)S(1)}, u32[]{:S(2)}, u32[]{:S(2)}) collective-permute-start(f32[8,16,256]{2,1,0:T(8,128)S(1)} %across_step.3), channel_id=1, source_target_pairs={{0,16},{4,20},{8,24},{12,28},{16,0},{20,4},{24,8},{28,12},{1,17},{... | collective-permute-start | bytes 393224 | tf_op jit(solution)/shard_map/ppermute | solution.py:331
  35.2 5.0 %collective-permute-start.6 = (f32[8,16,256]{2,1,0:T(8,128)S(1)}, f32[8,16,256]{2,1,0:T(8,128)S(1)}, u32[]{:S(2)}, u32[]{:S(2)}) collective-permute-start(f32[8,16,256]{2,1,0:T(8,128)S(1)} %get-tuple-element.67), channel_id=1, source_target_pairs={{0,8},{4,12},{8,0},{12,4},{16,24},{20,28},{24,16},{28,20},{1,9},{5... | collective-permute-start | bytes 393224 | tf_op jit(solution)/shard_map/ppermute | solution.py:331
  36.8 6.2 %collective-permute-start.11 = (f32[8,16,256]{2,1,0:T(8,128)S(1)}, f32[8,16,256]{2,1,0:T(8,128)S(1)}, u32[]{:S(2)}, u32[]{:S(2)}) collective-permute-start(f32[8,16,256]{2,1,0:T(8,128)S(1)} %get-tuple-element.72), channel_id=1, source_target_pairs={{0,4},{4,0},{8,12},{12,8},{16,20},{20,16},{24,28},{28,24},{1,5},{5... | collective-permute-start | bytes 393224 | tf_op jit(solution)/shard_map/ppermute | solution.py:331
  40.3 7.7 %copy-start.9 = (f32[512,128]{1,0:T(8,128)S(1)}, f32[512,128]{1,0:T(8,128)}, u32[]{:S(2)}) copy-start(f32[512,128]{1,0:T(8,128)} %copy-done.8) | copy-start | bytes 786436
  40.3 5.0 %collective-permute-start.7 = (f32[8,16,256]{2,1,0:T(8,128)S(1)}, f32[8,16,256]{2,1,0:T(8,128)S(1)}, u32[]{:S(2)}, u32[]{:S(2)}) collective-permute-start(f32[8,16,256]{2,1,0:T(8,128)S(1)} %pad_maximum_fusion), channel_id=1, source_target_pairs={{0,4},{4,0},{8,12},{12,8},{16,20},{20,16},{24,28},{28,24},{1,5},{5... | collective-permute-start | bytes 393224 | tf_op jit(solution)/shard_map/ppermute | solution.py:331
  43.0 5.0 %collective-permute-start.12 = (f32[8,16,256]{2,1,0:T(8,128)S(1)}, f32[8,16,256]{2,1,0:T(8,128)S(1)}, u32[]{:S(2)}, u32[]{:S(2)}) collective-permute-start(f32[8,16,256]{2,1,0:T(8,128)S(1)} %pad_maximum_fusion.2), channel_id=1, source_target_pairs={{0,8},{4,12},{8,0},{12,4},{16,24},{20,28},{24,16},{28,20},{1,9},{5... | collective-permute-start | bytes 393224 | tf_op jit(solution)/shard_map/ppermute | solution.py:331
  49.3 1.7 %collective-permute-start.13 = (f32[2,2,128,128]{3,2,1,0:T(8,128)}, f32[2,2,128,128]{3,2,1,0:T(8,128)S(1)}, u32[]{:S(2)}, u32[]{:S(2)}) collective-permute-start(f32[2,2,128,128]{3,2,1,0:T(8,128)} %get-tuple-element.82), channel_id=1, source_target_pairs={{0,1},{1,0},{2,3},{3,2},{4,5},{5,4},{6,7},{7,6},{8,9},{9,8},{10,11... | collective-permute-start | bytes 786440 | tf_op jit(solution)/shard_map/ppermute | solution.py:331
  49.3 4.6 %collective-permute-start.15 = (f32[2,2,128,128]{3,2,1,0:T(8,128)}, f32[2,2,128,128]{3,2,1,0:T(8,128)S(1)}, u32[]{:S(2)}, u32[]{:S(2)}) collective-permute-start(f32[2,2,128,128]{3,2,1,0:T(8,128)} %get-tuple-element.84), channel_id=1, source_target_pairs={{0,1},{1,0},{2,3},{3,2},{4,5},{5,4},{6,7},{7,6},{8,9},{9,8},{10,11... | collective-permute-start | bytes 786440 | tf_op jit(solution)/shard_map/ppermute | solution.py:331
  51.1 5.8 %collective-permute-start.14 = (f32[2,128,128]{2,1,0:T(8,128)S(1)}, f32[2,128,128]{2,1,0:T(8,128)S(1)}, u32[]{:S(2)}, u32[]{:S(2)}) collective-permute-start(f32[2,128,128]{2,1,0:T(8,128)S(1)} %dynamic-slice_bitcast_fusion.1), channel_id=1, source_target_pairs={{0,2},{1,3},{2,0},{3,1},{4,6},{5,7},{6,4},{7,5},{8,10},{9,11},{10,... | collective-permute-start | bytes 393224 | tf_op jit(solution)/shard_map/ppermute | solution.py:331
  54.0 5.5 %collective-permute-start.16 = (f32[2,128,128]{2,1,0:T(8,128)S(1)}, f32[2,128,128]{2,1,0:T(8,128)S(1)}, u32[]{:S(2)}, u32[]{:S(2)}) collective-permute-start(f32[2,128,128]{2,1,0:T(8,128)S(1)} %dynamic-slice_bitcast_fusion), channel_id=1, source_target_pairs={{0,2},{1,3},{2,0},{3,1},{4,6},{5,7},{6,4},{7,5},{8,10},{9,11},{10,... | collective-permute-start | bytes 393224 | tf_op jit(solution)/shard_map/ppermute | solution.py:331
  (6 other events, 5.4 us)

commit v2 on v1

--- a/solution.py
+++ b/solution.py
@@ -11,6 +11,8 @@
 MIDS = 6
 PARENTS = ROOTS + MIDS
 BLOCK = 128
+TILE = 8
+LOCAL_VMEM = 60 * 1024 * 1024
 F32 = jnp.float32
 BF16 = jnp.bfloat16
 
@@ -35,16 +37,13 @@
     return (row == seg * heads + col).astype(BF16)
 
 
-def rows_of(chain, order, rel, count):
-    me = lax.axis_index("seg")
-    first = jnp.bitwise_and(jnp.right_shift(me, order[0]), 1)
-    second = jnp.bitwise_and(jnp.right_shift(me, order[1]), 1)
-    part = jnp.bitwise_xor(first * 2 + second, rel)
-    return pl.multiple_of((chain * 4 + part) * count, count)
-
-
-def local_kernel(orders, in_hbm, cot_hbm, sin_hbm, sout_hbm, decay_hbm,
-                 scin_ref, sccot_ref, cum_ref, toend_ref, decays_ref, *refs):
+def quarter_of(distance, count):
+    place = jnp.bitwise_and(jnp.bitwise_xor(lax.axis_index("seg"), distance), 3)
+    return pl.multiple_of(place * count, count)
+
+
+def local_kernel(in_hbm, cot_hbm, sin_hbm, sout_hbm, decay_hbm,
+                 scin_ref, sccot_ref, cum_ref, toend_ref, *refs):
     states_s, in_ref, cot_ref, sin_ref, sout_ref, decay_ref, sems = refs[-7:]
     copies = [
         pltpu.make_async_copy(src, dst, sems.at[i])
@@ -79,9 +78,14 @@
     cum_ref[...] = cum
     row = lax.broadcasted_iota(jnp.int32, (rows, width), 0)
     col = lax.broadcasted_iota(jnp.int32, (rows, width), 1) // (width // heads)
+    tail = refs[0].shape[0] - TILE
     for s in range(segs):
         of_head = jnp.where(row == s * heads + col, jnp.exp(before), 0.0)
-        decays_ref[s:s + 1] = jnp.sum(of_head, axis=0, keepdims=True)
+        of_head = jnp.sum(of_head, axis=0, keepdims=True)
+        for ref in refs[:4]:
+            ref[tail + s:tail + s + 1] = of_head
+    for ref in refs[:4]:
+        ref[tail + segs:] = jnp.zeros((TILE - segs, width), F32)
     to_end = two_parts(jnp.exp(before - cum))
     toend_ref[...] = to_end
     from_start = two_parts(jnp.exp(cum))
@@ -95,13 +99,11 @@
         copies[2 * i + 2].wait()
         for s in range(segs):
             states_s[i * segs + s] = dot(state_ref[s], scaled_ref[s], TN)
-    for c, order in enumerate(orders):
-        near_ref, away_ref = refs[2 * c:2 * c + 2]
-        count = near_ref.shape[2]
-        for rel in range(4):
-            place = rows_of(c, order, rel, count)
-            for i in range(2 * segs):
-                (near_ref, away_ref)[rel // 2][rel % 2, i] = states_s[i, pl.ds(place, count)]
+    count = states_s.shape[1] // 4
+    for distance, ref in enumerate(refs[:4]):
+        place = quarter_of(distance, count)
+        for i in range(2 * segs):
+            ref[i * count:(i + 1) * count] = states_s[i, pl.ds(place, count)]
 
 
 def quad_kernel(seg, heads, in_ref, cot_ref, sin_ref, sout_ref, cum_ref, quad_ref, write_ref, read_ref):
@@ -151,7 +153,6 @@
     width = near_ref.shape[2]
     group = near_ref.shape[0]
     segs = group // 4
-    count = slots_ref.shape[0] // segs
     me = lax.axis_index("seg")
 
     def note(j, carry):
@@ -178,8 +179,7 @@
         above.append(up)
         top.append(jnp.where(up >= 0, parents_ref[known], -1))
         away = jnp.bitwise_xor(owner_s[known], me)
-        low, mid = jnp.bitwise_and(away, 1), jnp.bitwise_and(jnp.right_shift(away, 1), 1)
-        row = (mid * (count // 2) + low * (count // 4) + jnp.right_shift(away, 2)) * segs + slot_s[known]
+        row = away * segs + slot_s[known]
         at_ref[j:j + 1] = jnp.broadcast_to(row.astype(jnp.int32), (1, width))
     for j in range(group):
         for p in range(PARENTS):
@@ -197,8 +197,13 @@
             put(flag_ref, step_count + k, p, high == 1)
 
 
-def parent_decays(at_ref, decay_refs):
-    decays = jnp.concatenate([ref[...] for ref in decay_refs], axis=0)
+def group_decays(raws, into, at, segs):
+    tail = raws[0].shape[0] - TILE
+    for place, ref in enumerate(raws):
+        into[at + place * segs:at + (place + 1) * segs] = ref[tail:tail + segs]
+
+
+def parent_decays(at_ref, decays):
     row = lax.broadcasted_iota(jnp.int32, decays.shape, 0)
     return [
         jnp.sum(jnp.where(row == at_ref[j:j + 1], decays, 0.0), axis=0, keepdims=True)
@@ -206,30 +211,25 @@
     ]
 
 
-def raw_states(order, near_ref, first_ref, second_ref, segs, count):
-    ends, adjs = [None] * (4 * segs), [None] * (4 * segs)
-    for place, device in enumerate((0, 1 << order[0], 1 << order[1], 3)):
-        for s in range(segs):
-            for kind, found in ((0, ends), (1, adjs)):
-                i = kind * segs + s
-                if place < 2:
-                    value = (near_ref, first_ref)[place][0, i]
-                else:
-                    at = ((place - 2) * 2 * segs + i) * count
-                    value = second_ref[at:at + count]
-                found[device * segs + s] = value
+def raw_states(raws, segs, count):
+    ends = [ref[s * count:(s + 1) * count] for ref in raws for s in range(segs)]
+    adjs = [ref[(segs + s) * count:(segs + s + 1) * count] for ref in raws for s in range(segs)]
     return ends, adjs
 
 
-def cross_kernel(order, step, near_p, grand_p, hold_p, flag_ref, at_ref, mine_ref, tail_ref,
-                 near_ref, first_ref, second_ref, *refs):
-    later, out_ref = refs[:-1], refs[-1]
+def cross_kernel(step, carried, near_p, grand_p, hold_p, flag_ref, at_ref, *refs):
+    raws, later, out_ref = refs[:4], refs[4:-1], refs[-1]
     group = near_p.shape[0]
     segs = group // 4
-    count = out_ref.shape[1]
+    count = out_ref.shape[0] // (PARENTS * TILE) * TILE
     steps = flag_ref.shape[0] // 2
-    decay = parent_decays(at_ref, (mine_ref, tail_ref))
-    ends, adjs = raw_states(order, near_ref, first_ref, second_ref, segs, count)
+    if carried:
+        group_decays(raws, out_ref, PARENTS * count, segs)
+        decay = parent_decays(at_ref, out_ref[PARENTS * count:PARENTS * count + group])
+    else:
+        decay = parent_decays(at_ref, later[0][...])
+        later = later[1:]
+    ends, adjs = raw_states(raws, segs, count)
     as_end = flag_ref[step]
     from_end = [as_end * hold_p[j] for j in range(group)]
     from_adj = [(1.0 - as_end) * (near_p[j] + grand_p[j] * decay[j]) for j in range(group)]
@@ -241,57 +241,65 @@
         for j in range(group):
             value += from_end[j][p:p + 1] * ends[j] + from_adj[j][p:p + 1] * adjs[j]
         for flag, got in zip(passed, later):
-            value += flag[p:p + 1] * got[p]
-        out_ref[p] = value
-
-
-def finish_kernel(order, near_p, grand_p, hold_p, up_ref, far_ref, flag_ref, at_ref, mine_ref, tail_ref,
-                  near_ref, first_ref, second_ref, *refs):
-    later, (own_ref, there_ref, away_ref) = refs[:-3], refs[-3:]
+            value += flag[p:p + 1] * got[p * count:(p + 1) * count]
+        out_ref[p * count:(p + 1) * count] = value
+
+
+def finish_kernel(carried, near_p, grand_p, hold_p, up_ref, far_ref, flag_ref, at_ref, *refs):
+    raws, refs = refs[:4], refs[4:]
+    outs, decays_s = refs[-5:-1], refs[-1]
+    later = refs[:-5]
     group = near_p.shape[0]
     segs = group // 4
-    count = own_ref.shape[1]
+    count = outs[0].shape[0] // (2 * segs)
     steps = flag_ref.shape[0] // 2
-    decay = parent_decays(at_ref, (mine_ref, tail_ref))
-    ends, adjs = raw_states(order, near_ref, first_ref, second_ref, segs, count)
+    if carried:
+        group_decays(raws, decays_s, 0, segs)
+        decays_s[group:] = later[0][PARENTS * count:PARENTS * count + group]
+        decay = parent_decays(at_ref, decays_s[...])
+    else:
+        decay = parent_decays(at_ref, later[0][...])
+        later = later[1:]
+    ends, adjs = raw_states(raws, segs, count)
     values, known = [], []
     for p in range(PARENTS):
         value, end = 0.0, 0.0
         for j, got in enumerate(later):
-            value += got[p]
-            end += flag_ref[steps + j, p:p + 1] * got[p]
+            part = got[p * count:(p + 1) * count]
+            value += part
+            end += flag_ref[steps + j, p:p + 1] * part
         values.append(value)
         known.append(end)
     link = [up_ref[j] + far_ref[j] * decay[j] for j in range(group)]
-    for place, device in enumerate((0, 1 << order[0], 1 << order[1], 3)):
-        out_ref, base = ((own_ref, 0), (there_ref, 0), (away_ref, 0), (away_ref, 2 * segs))[place]
-        for s in range(segs):
-            j = device * segs + s
-            weight = near_p[j] + grand_p[j] * decay[j]
-            start, adj = 0.0, 0.0
+    for j in range(group):
+        weight = near_p[j] + grand_p[j] * decay[j]
+        takes = hold_p[j]
+        if carried:
             for i in range(group):
-                start += link[j][i:i + 1] * ends[i]
-                adj += link[i][j:j + 1] * adjs[i]
-            for p in range(PARENTS):
-                start += weight[p:p + 1] * known[p]
-                adj += hold_p[j, p:p + 1] * values[p]
-            out_ref[base + s] = start
-            out_ref[base + segs + s] = adj
-
-
-def state_kernel(orders, scin_ref, sccot_ref, *refs):
-    parts, refs = refs[:3 * len(orders)], refs[3 * len(orders):]
+                takes += (up_ref[i, j:j + 1] * decays_s[i:i + 1]) * hold_p[i]
+        start, adj = 0.0, 0.0
+        for i in range(group):
+            start += link[j][i:i + 1] * ends[i]
+            adj += link[i][j:j + 1] * adjs[i]
+        for p in range(PARENTS):
+            start += weight[p:p + 1] * known[p]
+            adj += takes[p:p + 1] * values[p]
+        out_ref, s = outs[j // segs], j % segs
+        out_ref[s * count:(s + 1) * count] = start
+        out_ref[(segs + s) * count:(segs + s + 1) * count] = adj
+
+
+def state_kernel(scin_ref, sccot_ref, *refs):
+    parts, refs = refs[:4], refs[4:]
     segs = scin_ref.shape[0]
     quads, refs = refs[:2 * segs], refs[2 * segs:]
     keep_w, send_w, keep_r, send_r, adj_out, start_s, total_s = refs
-    for c, order in enumerate(orders):
-        own, fourth, fifth = parts[3 * c:3 * c + 3]
-        count = own.shape[1]
-        for rel, (ref, base) in enumerate(((own, 0), (fourth, 0), (fifth, 0), (fifth, 2 * segs))):
-            place = rows_of(c, order, rel, count)
-            for s in range(segs):
-                start_s[s, pl.ds(place, count)] = ref[base + s].astype(BF16)
-                adj_out[s, pl.ds(place, count)] = ref[base + segs + s].astype(BF16)
+    count = parts[0].shape[0] // (2 * segs)
+    for distance, ref in enumerate(parts):
+        place = quarter_of(distance, count)
+        for s in range(segs):
+            start_s[s, pl.ds(place, count)] = ref[s * count:(s + 1) * count].astype(BF16)
+            adj_out[s, pl.ds(place, count)] = ref[(segs + s) * count:(segs + s + 1) * count].astype(BF16)
     bit = lax.axis_index("head") % 2
     piece = keep_w.shape[2]
     for a, (scaled, table, keep_ref, send_ref) in enumerate(
@@ -334,46 +342,8 @@
 PARAMS = pltpu.CompilerParams(vmem_limit_bytes=48 * 1024 * 1024)
 
 
-def close_decays(decays, count):
-    bits = count.bit_length() - 1
-    if bits == 3:
-        other, across, both = (
-            lax.ppermute(decays, "seg", [(i, i ^ k) for i in range(count)]) for k in (1, 4, 5)
-        )
-        return jnp.concatenate([decays, across, other, both], axis=0)
-    for bit in range(2, bits):
-        decays = jnp.concatenate([decays, flip(decays, "seg", count, bit)], axis=0)
-    return jnp.concatenate([decays, flip(decays, "seg", count, 0)], axis=0)
-
-
-def tree_chain(order, count, plan, decays, near, near_late, first, second):
-    near_p, grand_p, hold_p, up, far, flags, at = plan
-    shape = near.shape[1:]
-    part = jax.ShapeDtypeStruct(shape, F32)
-    later = []
-    for k in range(2, len(order)):
-        send = pl.pallas_call(
-            functools.partial(cross_kernel, order, k - 2),
-            out_shape=jax.ShapeDtypeStruct((PARENTS, *shape[1:]), F32),
-            in_specs=[in_vmem()] * (10 + len(later)),
-            out_specs=in_vmem(),
-            compiler_params=PARAMS,
-            cost_estimate=pl.CostEstimate(flops=2_000_000, bytes_accessed=500_000, transcendentals=0),
-            name="across_step",
-        )(near_p, grand_p, hold_p, flags, at, *decays, near, first, second, *later)
-        later.append(flip(send, "seg", count, order[k]))
-    own, there, away = pl.pallas_call(
-        functools.partial(finish_kernel, order),
-        out_shape=(part, part, jax.ShapeDtypeStruct((2 * shape[0], *shape[1:]), F32)),
-        in_specs=[in_vmem()] * (12 + len(later)),
-        out_specs=(in_vmem(), in_vmem(), in_vmem()),
-        compiler_params=PARAMS,
-        cost_estimate=pl.CostEstimate(flops=2_000_000, bytes_accessed=500_000, transcendentals=0),
-        name="finish_part",
-    )(near_p, grand_p, hold_p, up, far, flags, at, *decays, near_late, first, second, *later)
-    fourth = flip(away, "seg", count, order[1])
-    fifth = flip(jnp.concatenate([there, fourth[shape[0]:]], axis=0), "seg", count, order[0])
-    return own, fourth, fifth
+def to_distance(x, count, distance):
+    return lax.ppermute(x, "seg", [(i, i ^ distance) for i in range(count)])
 
 
 def shards(mesh_sizes, inputs, cotangent, state_in, state_out, log_decay, parents, slot_segment):
@@ -384,24 +354,22 @@
     heads = log_decay.shape[1]
     state = state_in.shape[2]
     rows = segs * heads
-    orders = [[0, 1] + list(range(2, bit_count)), [1, 0] + list(range(2, bit_count))]
-    part_rows = state // (4 * len(orders))
-
-    whole_in = whole(segs, length, width)
-    whole_state = whole(segs, length, state)
+    quarter = state // 4
+    group = 4 * segs
+    steps = bit_count - 2
+
     scaled = jax.ShapeDtypeStruct((segs, length, width), BF16)
-    raw = jax.ShapeDtypeStruct((2, 2 * segs, part_rows, width), F32)
-    scaled_in, scaled_cot, cum, to_end, decays, *raws = pl.pallas_call(
-        functools.partial(local_kernel, orders),
+    raw = jax.ShapeDtypeStruct((2 * segs * quarter + TILE, width), F32)
+    scaled_in, scaled_cot, cum, to_end, *raws = pl.pallas_call(
+        local_kernel,
         out_shape=(
             scaled, scaled,
             jax.ShapeDtypeStruct((rows, length), F32),
             jax.ShapeDtypeStruct((2 * rows, length), BF16),
-            jax.ShapeDtypeStruct((segs, width), F32),
-            *[raw] * (2 * len(orders)),
+            *[raw] * 4,
         ),
         in_specs=[pl.BlockSpec(memory_space=pltpu.HBM)] * 5,
-        out_specs=tuple([in_vmem()] * (5 + 2 * len(orders))),
+        out_specs=tuple([in_vmem()] * 8),
         scratch_shapes=[
             pltpu.VMEM((2 * segs, state, width), F32),
             pltpu.VMEM(inputs.shape, BF16),
@@ -411,11 +379,12 @@
             pltpu.VMEM(log_decay.shape, F32),
             pltpu.SemaphoreType.DMA((5,)),
         ],
-        compiler_params=PARAMS,
+        compiler_params=pltpu.CompilerParams(vmem_limit_bytes=LOCAL_VMEM),
         cost_estimate=pl.CostEstimate(flops=200_000_000, bytes_accessed=4_000_000, transcendentals=8192),
         name="local_states",
     )(inputs, cotangent, state_in, state_out, log_decay)
-    nears, aways = raws[0::2], raws[1::2]
+
+    group_raws = [raws[0]] + [to_distance(raws[d], count, d) for d in range(1, 4)]
 
     quads = []
     for s in range(segs):
@@ -445,27 +414,13 @@
             )(inputs, cotangent, state_in, state_out, cum)
         )
 
-    firsts = [flip(away, "seg", count, order[0]) for away, order in zip(aways, orders)]
-    mine = close_decays(decays, count)
-    held, quads[0] = lax.optimization_barrier((nears[0], quads[0]))
-    late, quads[1:] = lax.optimization_barrier((nears[0], quads[1:]))
-    raw_rows = 2 * segs * part_rows
-    seconds = []
-    for c, order in enumerate(orders):
-        message = [(held if c == 0 else nears[c])[1].reshape(raw_rows, width), firsts[c][1].reshape(raw_rows, width)]
-        if c == 0:
-            message.append(mine)
-        seconds.append(flip(jnp.concatenate(message, axis=0), "seg", count, order[1]))
-    decays = (mine, seconds[0][2 * raw_rows:])
-
-    group = 4 * segs
     by_parent = jax.ShapeDtypeStruct((group, PARENTS, width), F32)
     by_segment = jax.ShapeDtypeStruct((group, group, width), F32)
     plan = pl.pallas_call(
-        functools.partial(plan_kernel, bit_count - 2),
+        functools.partial(plan_kernel, steps),
         out_shape=(
             by_parent, by_parent, by_parent, by_segment, by_segment,
-            jax.ShapeDtypeStruct((2 * (bit_count - 2), PARENTS, width), F32),
+            jax.ShapeDtypeStruct((2 * steps, PARENTS, width), F32),
             jax.ShapeDtypeStruct((group, width), jnp.int32),
         ),
         in_specs=[in_smem(), in_smem()],
@@ -476,15 +431,48 @@
         name="plan_tree",
     )(parents, slot_segment)
 
-    parts = []
-    for c, order in enumerate(orders):
-        last = late if c == 0 else nears[c]
-        parts.extend(tree_chain(order, count, plan, decays, nears[c], last, firsts[c], seconds[c]))
+    own, quads[0] = lax.optimization_barrier((raws[0], quads[0]))
+    own_late, quads[1:] = lax.optimization_barrier((raws[0], quads[1:]))
+    near_p, grand_p, hold_p, up, far, flags, at = plan
+
+    carried = steps == 1
+    decays = []
+    if not carried:
+        known = raws[0][2 * segs * quarter:2 * segs * quarter + segs]
+        for bit in range(bit_count):
+            known = jnp.concatenate([known, to_distance(known, count, 1 << bit)], axis=0)
+        decays = [known]
+    later = []
+    for k in range(steps):
+        message = (PARENTS * quarter + (TILE if carried else 0), width)
+        send = pl.pallas_call(
+            functools.partial(cross_kernel, k, carried),
+            out_shape=jax.ShapeDtypeStruct(message, F32),
+            in_specs=[in_vmem()] * (9 + len(decays) + len(later)),
+            out_specs=in_vmem(),
+            compiler_params=PARAMS,
+            cost_estimate=pl.CostEstimate(flops=2_000_000, bytes_accessed=500_000, transcendentals=0),
+            name="across_step",
+        )(near_p, grand_p, hold_p, flags, at, own, *group_raws[1:], *decays, *later)
+        later.append(to_distance(send, count, 4 << k))
+
+    part = jax.ShapeDtypeStruct((2 * segs * quarter, width), F32)
+    parts = pl.pallas_call(
+        functools.partial(finish_kernel, carried),
+        out_shape=(part, part, part, part),
+        in_specs=[in_vmem()] * (11 + len(decays) + len(later)),
+        out_specs=tuple([in_vmem()] * 4),
+        scratch_shapes=[pltpu.VMEM((2 * group, width), F32)],
+        compiler_params=PARAMS,
+        cost_estimate=pl.CostEstimate(flops=2_000_000, bytes_accessed=500_000, transcendentals=0),
+        name="finish_states",
+    )(near_p, grand_p, hold_p, up, far, flags, at, own_late, *group_raws[1:], *decays, *later)
+    parts = [parts[0]] + [to_distance(parts[d], count, d) for d in range(1, 4)]
 
     piece = length // head_devices
     half = jax.ShapeDtypeStruct((2, segs, piece, state), F32)
     keep_w, send_w, keep_r, send_r, adj_all = pl.pallas_call(
-        functools.partial(state_kernel, orders),
+        state_kernel,
         out_shape=(half, half, half, half, jax.ShapeDtypeStruct((segs, state, width), BF16)),
         in_specs=[in_vmem()] * (2 + len(parts) + 2 * segs),
         out_specs=tuple([in_vmem()] * 5),

time: 60.5 us -> 51.4 us (0.85)
  starting transfers between devices: 19.3 us -> 13.8 us
  local copies, waits for them, and re-layouts: 5.39 us -> 1.44 us
    ppermute x14 -> x4, waiting for transfers between devices: 22.4 us -> 5.23 us  [flip(): return lax.ppermute(x, axis, [(i, i ^ 1 << bit) for i in range(count)])]
    ppermute x3 -> x7, waiting for transfers between devices: 0.01 us -> 16.9 us  [to_distance(): return lax.ppermute(x, 'seg', [(i, i ^ distance) for i in range(count)])]
    ppermute x14 -> x4, starting transfers between devices: 13.6 us -> 2.79 us  [flip(): return lax.ppermute(x, axis, [(i, i ^ 1 << bit) for i in range(count)])]
    ppermute x3 -> x7, starting transfers between devices: 5.7 us -> 11 us  [to_distance(): return lax.ppermute(x, 'seg', [(i, i ^ distance) for i in range(count)])]
    unnamed x26 -> x24, local copies, waits for them, and re-layouts: 5.29 us -> 1.41 us
    pallas_call x7 -> x5, Pallas kernels: 5.53 us -> 6.19 us  [the longest x1 3.34 us: shards(): pl.pallas_call(local_kernel, out_shape=(scaled, scaled, jax.ShapeDtypeStr...]
  transfers between devices with their start and end apart: 17 -> 11, of which waited for: 10 -> 9; matrix products, arithmetic and copies ran while one was open for 1% -> 1% of each run, Pallas kernels for 13% -> 13%
where the time goes in v2:
time: 51.4 us; the launch traced here: 51 us
  waiting for transfers between devices  22.2 us (43%)
  starting transfers between devices  13.8 us (27%)
  Pallas kernels  11.4 us (22%)
  local copies, waits for them, and re-layouts  1.44 us (3%)
  other arithmetic  1.4 us (3%)
  between operations  0.81 us (2%)
    ppermute x7, waiting for transfers between devices, to_distance(): return lax.ppermute(x, 'seg', [(i, i ^ distance) for i in range(count)])  16.9 us
    ppermute x7, starting transfers between devices, to_distance(): return lax.ppermute(x, 'seg', [(i, i ^ distance) for i in range(count)])  11 us
    ppermute x4, waiting for transfers between devices, flip(): return lax.ppermute(x, axis, [(i, i ^ 1 << bit) for i in range(count)])  5.23 us
    pallas_call x2, Pallas kernels, shards(): pl.pallas_call(functools.partial(quad_kernel, s, heads), grid=(1,), out_s...  3.99 us
    pallas_call x1, Pallas kernels, shards(): pl.pallas_call(local_kernel, out_shape=(scaled, scaled, jax.ShapeDtypeStr...  3.34 us
    ppermute x4, starting transfers between devices, flip(): return lax.ppermute(x, axis, [(i, i ^ 1 << bit) for i in range(count)])  2.79 us
    unnamed x24, local copies, waits for them, and re-layouts  1.41 us
    add x2, other arithmetic, shards(): outs.append(here + flip(away, 'head', head_devices, 1))  1.34 us
  transfers between devices with their start and end apart: 11, of which 9 were waited for; matrix products, arithmetic and copies ran while one was open for 1% of the time, Pallas kernels for 13%

profile of v2, /device:TPU:0, one launch (start us, length us, event | category | flops | bytes accessed | tf_op | source)
XLA Modules:
  0.0 51.0 jit_solution(14109523998672905642)
XLA Ops:
  0.7 3.3 %local_states.1 = (bf16[2,512,256]{2,1,0:T(8,128)(2,1)}, bf16[2,512,256]{2,1,0:T(8,128)(2,1)}, f32[8,512]{1,0:T(8,128)}, bf16[16,512]{1,0:T(8,128)(2,1)}, f32[13...) custom-call(bf16[2,512,256]{2,1,0:T(8,128)(2,1)} %in_ref.3, ...), custom_call_target="tpu_custom_call" | custom-call | flops 200000000 | bytes 4000000 | tf_op jit(solution)/shard_map/local_states/pallas_call | solution.py:363
  4.0 3.0 %collective-permute-start = (f32[136,256]{1,0:T(8,128)}, f32[136,256]{1,0:T(8,128)S(1)}, u32[]{:S(2)}, u32[]{:S(2)}) collective-permute-start(f32[136,256]{1,0:T(8,128)} %get-tuple-element.57), channel_id=1, source_target_pairs={{0,4},{4,0},{8,12},{12,8},{16,20},{20,16},{24,28},{28,24},{1,5},{5... | collective-permute-start | bytes 417800 | tf_op jit(solution)/shard_map/ppermute | solution.py:346
  7.1 1.6 %collective-permute-start.1 = (f32[136,256]{1,0:T(8,128)}, f32[136,256]{1,0:T(8,128)S(1)}, u32[]{:S(2)}, u32[]{:S(2)}) collective-permute-start(f32[136,256]{1,0:T(8,128)} %get-tuple-element.58), channel_id=1, source_target_pairs={{0,8},{4,12},{8,0},{12,4},{16,24},{20,28},{24,16},{28,20},{1,9},{5... | collective-permute-start | bytes 417800 | tf_op jit(solution)/shard_map/ppermute | solution.py:346
  8.7 0.7 %copy-done.8 = f32[8,512]{1,0:T(8,128)S(1)} copy-done((f32[8,512]{1,0:T(8,128)S(1)}, f32[8,512]{1,0:T(8,128)}, u32[]{:S(2)}) %copy-start.8) | copy-done | bytes 16408
  9.4 2.0 %quadratic_part.3 = (f32[512,256]{1,0:T(8,128)S(1)}, f32[512,128]{1,0:T(8,128)S(1)}, f32[512,128]{1,0:T(8,128)S(1)}) custom-call(bf16[2,512,256]{2,1,0:T(8,128)(2,1)S(1)} %copy-done.2, bf16[2,512,256]{2,1,0:T(8,128)(2,1)S(1)} %copy-done.3, bf16[2,512,128]{2,1,0:T(8,128)(2,1)S(1)} %copy-done, bf16[2,512,128]{2,1,0:T(8,128)(2,1)S(1)} %copy-done.6, ...), custom_call_target="tpu_custom_call" | custom-call | flops 4000000000 | bytes 2000000 | tf_op jit(solution)/shard_map/quadratic_part/pallas_call | solution.py:393
  12.1 1.1 %plan_tree.1 = (f32[8,8,256]{2,1,0:T(8,128)S(1)}, f32[8,8,256]{2,1,0:T(8,128)S(1)}, f32[8,8,256]{2,1,0:T(8,128)S(1)}, f32[8,8,256]{2,1,0:T(8,128)S(1)}, f32[8,8,...) custom-call(s32[16]{0:T(128)S(1)} %copy-done.10, s32[16]{0:T(128)S(1)} %copy-done.11), custom_call_target="tpu_custom_call" | custom-call | flops 2000000 | bytes 500000 | tf_op jit(solution)/shard_map/plan_tree/pallas_call | solution.py:419
  13.9 1.3 %collective-permute-done.2.refs_3_ = f32[136,256]{1,0:T(8,128)S(1)} collective-permute-done((f32[136,256]{1,0:T(8,128)}, f32[136,256]{1,0:T(8,128)S(1)}, u32[]{:S(2)}, u32[]{:S(2)}) %collective-permute-start.2) | collective-permute-done | bytes 139296 | tf_op jit(solution)/shard_map/ppermute | solution.py:346
  15.5 2.8 %collective-permute-start.3 = (f32[264,256]{1,0:T(8,128)S(1)}, f32[264,256]{1,0:T(8,128)S(1)}, u32[]{:S(2)}, u32[]{:S(2)}) collective-permute-start(f32[264,256]{1,0:T(8,128)S(1)} %across_step.1), channel_id=1, source_target_pairs={{0,16},{4,20},{8,24},{12,28},{16,0},{20,4},{24,8},{28,12},{1,17},{... | collective-permute-start | bytes 811016 | tf_op jit(solution)/shard_map/ppermute | solution.py:346
  18.3 2.0 %quadratic_part.2 = (f32[512,256]{1,0:T(8,128)S(1)}, f32[512,128]{1,0:T(8,128)S(1)}, f32[512,128]{1,0:T(8,128)S(1)}) custom-call(bf16[2,512,256]{2,1,0:T(8,128)(2,1)S(1)} %copy-done.2, bf16[2,512,256]{2,1,0:T(8,128)(2,1)S(1)} %copy-done.3, bf16[2,512,128]{2,1,0:T(8,128)(2,1)S(1)} %copy-done, bf16[2,512,128]{2,1,0:T(8,128)(2,1)S(1)} %copy-done.6, ...), custom_call_target="tpu_custom_call" | custom-call | flops 4000000000 | bytes 2000000 | tf_op jit(solution)/shard_map/quadratic_part/pallas_call | solution.py:393
  20.3 9.5 %collective-permute-done.3.refs_4_ = f32[264,256]{1,0:T(8,128)S(1)} collective-permute-done((f32[264,256]{1,0:T(8,128)S(1)}, f32[264,256]{1,0:T(8,128)S(1)}, u32[]{:S(2)}, u32[]{:S(2)}) %collective-permute-start.3) | collective-permute-done | bytes 270368 | tf_op jit(solution)/shard_map/ppermute | solution.py:346
  29.9 0.8 %finish_states.1 = (f32[128,256]{1,0:T(8,128)S(1)}, f32[128,256]{1,0:T(8,128)S(1)}, f32[128,256]{1,0:T(8,128)S(1)}, f32[128,256]{1,0:T(8,128)S(1)}) custom-call(f32[8,8,256]{2,1,0:T(8,128)S(1)} %get-tuple-element.44.near_p, f32[8,8,256]{2,1,0:T(8,128)S(1)} %get-tuple-element.45.grand_p, f32[8,8,256]{2,1,0:T(8,128)S(1)} %get-tuple-element.46.hold_p, ...), custom_call_target="tpu_custom_call" | custom-call | flops 2000000 | bytes 500000 | tf_op jit(solution)/shard_map/finish_states/pallas_call | solution.py:460
  30.6 1.2 %collective-permute-start.4 = (f32[128,256]{1,0:T(8,128)S(1)}, f32[128,256]{1,0:T(8,128)S(1)}, u32[]{:S(2)}, u32[]{:S(2)}) collective-permute-start(f32[128,256]{1,0:T(8,128)S(1)} %get-tuple-element.65), channel_id=1, source_target_pairs={{0,4},{4,0},{8,12},{12,8},{16,20},{20,16},{24,28},{28,24},{1,5},{5... | collective-permute-start | bytes 393224 | tf_op jit(solution)/shard_map/ppermute | solution.py:346
  31.8 0.7 %collective-permute-start.5 = (f32[128,256]{1,0:T(8,128)S(1)}, f32[128,256]{1,0:T(8,128)S(1)}, u32[]{:S(2)}, u32[]{:S(2)}) collective-permute-start(f32[128,256]{1,0:T(8,128)S(1)} %get-tuple-element.66), channel_id=1, source_target_pairs={{0,8},{4,12},{8,0},{12,4},{16,24},{20,28},{24,16},{28,20},{1,9},{5... | collective-permute-start | bytes 393224 | tf_op jit(solution)/shard_map/ppermute | solution.py:346
  32.5 1.7 %collective-permute-start.6 = (f32[128,256]{1,0:T(8,128)S(1)}, f32[128,256]{1,0:T(8,128)S(1)}, u32[]{:S(2)}, u32[]{:S(2)}) collective-permute-start(f32[128,256]{1,0:T(8,128)S(1)} %get-tuple-element.67), channel_id=1, source_target_pairs={{0,12},{4,8},{8,4},{12,0},{16,28},{20,24},{24,20},{28,16},{1,13},{... | collective-permute-start | bytes 393224 | tf_op jit(solution)/shard_map/ppermute | solution.py:346
  34.2 2.0 %collective-permute-done.4.refs_1_ = f32[128,256]{1,0:T(8,128)S(1)} collective-permute-done((f32[128,256]{1,0:T(8,128)S(1)}, f32[128,256]{1,0:T(8,128)S(1)}, u32[]{:S(2)}, u32[]{:S(2)}) %collective-permute-start.4) | collective-permute-done | bytes 131104 | tf_op jit(solution)/shard_map/ppermute | solution.py:346
  36.2 1.2 %collective-permute-done.5.refs_2_ = f32[128,256]{1,0:T(8,128)S(1)} collective-permute-done((f32[128,256]{1,0:T(8,128)S(1)}, f32[128,256]{1,0:T(8,128)S(1)}, u32[]{:S(2)}, u32[]{:S(2)}) %collective-permute-start.5) | collective-permute-done | bytes 131104 | tf_op jit(solution)/shard_map/ppermute | solution.py:346
  37.3 2.3 %collective-permute-done.6.refs_3_ = f32[128,256]{1,0:T(8,128)S(1)} collective-permute-done((f32[128,256]{1,0:T(8,128)S(1)}, f32[128,256]{1,0:T(8,128)S(1)}, u32[]{:S(2)}, u32[]{:S(2)}) %collective-permute-start.6) | collective-permute-done | bytes 131104 | tf_op jit(solution)/shard_map/ppermute | solution.py:346
  40.8 1.0 %collective-permute-done.7 = f32[2,2,128,128]{3,2,1,0:T(8,128)S(1)} collective-permute-done((f32[2,2,128,128]{3,2,1,0:T(8,128)S(1)}, f32[2,2,128,128]{3,2,1,0:T(8,128)S(1)}, u32[]{:S(2)}, u32[]{:S(2)}) %collective-permute-start.7) | collective-permute-done | bytes 262176 | tf_op jit(solution)/shard_map/ppermute | solution.py:339
  41.9 1.5 %collective-permute-start.8 = (f32[2,128,128]{2,1,0:T(8,128)S(1)}, f32[2,128,128]{2,1,0:T(8,128)S(1)}, u32[]{:S(2)}, u32[]{:S(2)}) collective-permute-start(f32[2,128,128]{2,1,0:T(8,128)S(1)} %dynamic-slice_bitcast_fusion.1), channel_id=1, source_target_pairs={{0,2},{1,3},{2,0},{3,1},{4,6},{5,7},{6,4},{7,5},{8,10},{9,11},{10,... | collective-permute-start | bytes 393224 | tf_op jit(solution)/shard_map/ppermute | solution.py:339
  43.5 1.3 %grad_inputs.1 = bf16[2,512,256]{2,1,0:T(8,128)(2,1)} custom-call(bf16[2,512,128]{2,1,0:T(8,128)(2,1)S(1)} %copy-done, bf16[16,512]{1,0:T(8,128)(2,1)S(1)} %copy-done.7, bf16[2,128,256]{2,1,0:T(8,128)(2,1)S(1)} %get-tuple-element.72.adj_ref, f32[512,256]{1,0:T(8,128)S(1)} %get-tuple-element.73.refs_0_, f32[512,256]{1,0:T(8,128)S(1)} %get-tuple-element.74.refs_1_), custom_call_target="tpu_custom_call" | custom-call | flops 200000000 | bytes 8000000 | tf_op jit(solution)/shard_map/grad_inputs/pallas_call | solution.py:488
  44.8 0.7 %collective-permute-start.10 = (f32[2,128,128]{2,1,0:T(8,128)S(1)}, f32[2,128,128]{2,1,0:T(8,128)S(1)}, u32[]{:S(2)}, u32[]{:S(2)}) collective-permute-start(f32[2,128,128]{2,1,0:T(8,128)S(1)} %dynamic-slice_bitcast_fusion), channel_id=1, source_target_pairs={{0,2},{1,3},{2,0},{3,1},{4,6},{5,7},{6,4},{7,5},{8,10},{9,11},{10,... | collective-permute-start | bytes 393224 | tf_op jit(solution)/shard_map/ppermute | solution.py:339
  45.5 2.2 %collective-permute-done.8 = f32[2,128,128]{2,1,0:T(8,128)S(1)} collective-permute-done((f32[2,128,128]{2,1,0:T(8,128)S(1)}, f32[2,128,128]{2,1,0:T(8,128)S(1)}, u32[]{:S(2)}, u32[]{:S(2)}) %collective-permute-start.8) | collective-permute-done | bytes 131104 | tf_op jit(solution)/shard_map/ppermute | solution.py:339
  47.7 0.7 %bitcast_add_fusion.1 = f32[2,128,128]{2,1,0:T(8,128)} fusion(f32[2,128,128]{2,1,0:T(8,128)S(1)} %collective-permute-done.8, f32[2,2,128,128]{3,2,1,0:T(8,128)S(1)} %add.23, s32[]{:T(128)S(6)} %select_n.15), kind=kLoop, calls=%fused_computation.1 | loop fusion | flops 32768 | bytes 393220 | tf_op jit(solution)/shard_map/add | solution.py:504
  48.4 2.0 %collective-permute-done.10 = f32[2,128,128]{2,1,0:T(8,128)S(1)} collective-permute-done((f32[2,128,128]{2,1,0:T(8,128)S(1)}, f32[2,128,128]{2,1,0:T(8,128)S(1)}, u32[]{:S(2)}, u32[]{:S(2)}) %collective-permute-start.10) | collective-permute-done | bytes 131104 | tf_op jit(solution)/shard_map/ppermute | solution.py:339
  (36 shorter events, 3.6 us)
Async XLA Ops:
  0.6 8.0 %copy-start = (bf16[2,512,128]{2,1,0:T(8,128)(2,1)S(1)}, bf16[2,512,128]{2,1,0:T(8,128)(2,1)}, u32[]{:S(2)}) copy-start(bf16[2,512,128]{2,1,0:T(8,128)(2,1)} %sin_ref.5) | copy-start | bytes 786436
  0.6 8.0 %copy-start.2 = (bf16[2,512,256]{2,1,0:T(8,128)(2,1)S(1)}, bf16[2,512,256]{2,1,0:T(8,128)(2,1)}, u32[]{:S(2)}) copy-start(bf16[2,512,256]{2,1,0:T(8,128)(2,1)} %in_ref.3) | copy-start | bytes 1572868
  0.7 8.0 %copy-start.3 = (bf16[2,512,256]{2,1,0:T(8,128)(2,1)S(1)}, bf16[2,512,256]{2,1,0:T(8,128)(2,1)}, u32[]{:S(2)}) copy-start(bf16[2,512,256]{2,1,0:T(8,128)(2,1)} %cot_ref.3) | copy-start | bytes 1572868
  0.7 8.0 %copy-start.6 = (bf16[2,512,128]{2,1,0:T(8,128)(2,1)S(1)}, bf16[2,512,128]{2,1,0:T(8,128)(2,1)}, u32[]{:S(2)}) copy-start(bf16[2,512,128]{2,1,0:T(8,128)(2,1)} %sout_ref.3) | copy-start | bytes 786436
  4.0 9.2 %collective-permute-start = (f32[136,256]{1,0:T(8,128)}, f32[136,256]{1,0:T(8,128)S(1)}, u32[]{:S(2)}, u32[]{:S(2)}) collective-permute-start(f32[136,256]{1,0:T(8,128)} %get-tuple-element.57), channel_id=1, source_target_pairs={{0,4},{4,0},{8,12},{12,8},{16,20},{20,16},{24,28},{28,24},{1,5},{5... | collective-permute-start | bytes 417800 | tf_op jit(solution)/shard_map/ppermute | solution.py:346
  7.1 6.8 %collective-permute-start.1 = (f32[136,256]{1,0:T(8,128)}, f32[136,256]{1,0:T(8,128)S(1)}, u32[]{:S(2)}, u32[]{:S(2)}) collective-permute-start(f32[136,256]{1,0:T(8,128)} %get-tuple-element.58), channel_id=1, source_target_pairs={{0,8},{4,12},{8,0},{12,4},{16,24},{20,28},{24,16},{28,20},{1,9},{5... | collective-permute-start | bytes 417800 | tf_op jit(solution)/shard_map/ppermute | solution.py:346
  8.6 6.5 %collective-permute-start.2 = (f32[136,256]{1,0:T(8,128)}, f32[136,256]{1,0:T(8,128)S(1)}, u32[]{:S(2)}, u32[]{:S(2)}) collective-permute-start(f32[136,256]{1,0:T(8,128)} %get-tuple-element.59), channel_id=1, source_target_pairs={{0,12},{4,8},{8,4},{12,0},{16,28},{20,24},{24,20},{28,16},{1,13},{... | collective-permute-start | bytes 417800 | tf_op jit(solution)/shard_map/ppermute | solution.py:346
  8.7 0.7 %copy-start.8 = (f32[8,512]{1,0:T(8,128)S(1)}, f32[8,512]{1,0:T(8,128)}, u32[]{:S(2)}) copy-start(f32[8,512]{1,0:T(8,128)} %get-tuple-element.52.cum_ref) | copy-start | bytes 49156
  9.4 5.8 %copy-start.1 = (f32[136,256]{1,0:T(8,128)S(1)}, f32[136,256]{1,0:T(8,128)}, u32[]{:S(2)}) copy-start(f32[136,256]{1,0:T(8,128)} %get-tuple-element.63.refs_0_) | copy-start | bytes 417796
  11.4 0.7 %copy-start.10 = (s32[16]{0:T(128)S(1)}, s32[16]{0:T(128)}, u32[]{:S(2)}) copy-start(s32[16]{0:T(128)} %parents_ref.1) | copy-start | bytes 196
  11.4 0.7 %copy-start.11 = (s32[16]{0:T(128)S(1)}, s32[16]{0:T(128)}, u32[]{:S(2)}) copy-start(s32[16]{0:T(128)} %slots_ref.1) | copy-start | bytes 196
  15.2 3.2 %copy-start.9 = (f32[8,512]{1,0:T(8,128)S(1)}, f32[8,512]{1,0:T(8,128)}, u32[]{:S(2)}) copy-start(f32[8,512]{1,0:T(8,128)} %get-tuple-element.52.cum_ref) | copy-start | bytes 49156
  15.5 14.3 %collective-permute-start.3 = (f32[264,256]{1,0:T(8,128)S(1)}, f32[264,256]{1,0:T(8,128)S(1)}, u32[]{:S(2)}, u32[]{:S(2)}) collective-permute-start(f32[264,256]{1,0:T(8,128)S(1)} %across_step.1), channel_id=1, source_target_pairs={{0,16},{4,20},{8,24},{12,28},{16,0},{20,4},{24,8},{28,12},{1,17},{... | collective-permute-start | bytes 811016 | tf_op jit(solution)/shard_map/ppermute | solution.py:346
  29.9 9.8 %copy-start.4 = (bf16[2,512,256]{2,1,0:T(8,128)(2,1)S(1)}, bf16[2,512,256]{2,1,0:T(8,128)(2,1)}, u32[]{:S(2)}) copy-start(bf16[2,512,256]{2,1,0:T(8,128)(2,1)} %get-tuple-element.42.scin_ref) | copy-start | bytes 1572868
  29.9 9.8 %copy-start.5 = (bf16[2,512,256]{2,1,0:T(8,128)(2,1)S(1)}, bf16[2,512,256]{2,1,0:T(8,128)(2,1)}, u32[]{:S(2)}) copy-start(bf16[2,512,256]{2,1,0:T(8,128)(2,1)} %get-tuple-element.43.sccot_ref) | copy-start | bytes 1572868
  30.6 5.5 %collective-permute-start.4 = (f32[128,256]{1,0:T(8,128)S(1)}, f32[128,256]{1,0:T(8,128)S(1)}, u32[]{:S(2)}, u32[]{:S(2)}) collective-permute-start(f32[128,256]{1,0:T(8,128)S(1)} %get-tuple-element.65), channel_id=1, source_target_pairs={{0,4},{4,0},{8,12},{12,8},{16,20},{20,16},{24,28},{28,24},{1,5},{5... | collective-permute-start | bytes 393224 | tf_op jit(solution)/shard_map/ppermute | solution.py:346
  31.8 5.5 %collective-permute-start.5 = (f32[128,256]{1,0:T(8,128)S(1)}, f32[128,256]{1,0:T(8,128)S(1)}, u32[]{:S(2)}, u32[]{:S(2)}) collective-permute-start(f32[128,256]{1,0:T(8,128)S(1)} %get-tuple-element.66), channel_id=1, source_target_pairs={{0,8},{4,12},{8,0},{12,4},{16,24},{20,28},{24,16},{28,20},{1,9},{5... | collective-permute-start | bytes 393224 | tf_op jit(solution)/shard_map/ppermute | solution.py:346
  32.5 7.2 %collective-permute-start.6 = (f32[128,256]{1,0:T(8,128)S(1)}, f32[128,256]{1,0:T(8,128)S(1)}, u32[]{:S(2)}, u32[]{:S(2)}) collective-permute-start(f32[128,256]{1,0:T(8,128)S(1)} %get-tuple-element.67), channel_id=1, source_target_pairs={{0,12},{4,8},{8,4},{12,0},{16,28},{20,24},{24,20},{28,16},{1,13},{... | collective-permute-start | bytes 393224 | tf_op jit(solution)/shard_map/ppermute | solution.py:346
  40.3 1.6 %collective-permute-start.7 = (f32[2,2,128,128]{3,2,1,0:T(8,128)S(1)}, f32[2,2,128,128]{3,2,1,0:T(8,128)S(1)}, u32[]{:S(2)}, u32[]{:S(2)}) collective-permute-start(f32[2,2,128,128]{3,2,1,0:T(8,128)S(1)} %get-tuple-element.76), channel_id=1, source_target_pairs={{0,1},{1,0},{2,3},{3,2},{4,5},{5,4},{6,7},{7,6},{8,9},{9,8},{10,11... | collective-permute-start | bytes 786440 | tf_op jit(solution)/shard_map/ppermute | solution.py:339
  40.3 4.4 %collective-permute-start.9 = (f32[2,2,128,128]{3,2,1,0:T(8,128)S(1)}, f32[2,2,128,128]{3,2,1,0:T(8,128)S(1)}, u32[]{:S(2)}, u32[]{:S(2)}) collective-permute-start(f32[2,2,128,128]{3,2,1,0:T(8,128)S(1)} %get-tuple-element.78), channel_id=1, source_target_pairs={{0,1},{1,0},{2,3},{3,2},{4,5},{5,4},{6,7},{7,6},{8,9},{9,8},{10,11... | collective-permute-start | bytes 786440 | tf_op jit(solution)/shard_map/ppermute | solution.py:339
  41.9 1.6 %copy-start.7 = (bf16[16,512]{1,0:T(8,128)(2,1)S(1)}, bf16[16,512]{1,0:T(8,128)(2,1)}, u32[]{:S(2)}) copy-start(bf16[16,512]{1,0:T(8,128)(2,1)} %get-tuple-element.41.toend_ref) | copy-start | bytes 49156
  41.9 5.8 %collective-permute-start.8 = (f32[2,128,128]{2,1,0:T(8,128)S(1)}, f32[2,128,128]{2,1,0:T(8,128)S(1)}, u32[]{:S(2)}, u32[]{:S(2)}) collective-permute-start(f32[2,128,128]{2,1,0:T(8,128)S(1)} %dynamic-slice_bitcast_fusion.1), channel_id=1, source_target_pairs={{0,2},{1,3},{2,0},{3,1},{4,6},{5,7},{6,4},{7,5},{8,10},{9,11},{10,... | collective-permute-start | bytes 393224 | tf_op jit(solution)/shard_map/ppermute | solution.py:339
  44.8 5.6 %collective-permute-start.10 = (f32[2,128,128]{2,1,0:T(8,128)S(1)}, f32[2,128,128]{2,1,0:T(8,128)S(1)}, u32[]{:S(2)}, u32[]{:S(2)}) collective-permute-start(f32[2,128,128]{2,1,0:T(8,128)S(1)} %dynamic-slice_bitcast_fusion), channel_id=1, source_target_pairs={{0,2},{1,3},{2,0},{3,1},{4,6},{5,7},{6,4},{7,5},{8,10},{9,11},{10,... | collective-permute-start | bytes 393224 | tf_op jit(solution)/shard_map/ppermute | solution.py:339
